TPU v7x, 32 devices: a whole 2x2x4 slice. The times are simulated.
32 devices in a mesh: samples: 2 (over x), brick: 16 (over z, y, core).
Axes of the slice: x: 2, y: 2, z: 4, core: 2. Of those that a mesh axis runs over, the one named last changes fastest.
Arguments:
- source: float32 [128, 128, 256], P(('samples', 'brick')), parts along dimension 0, may hold values from -6 to 6
- guess: float32 [128, 128, 256], P(('samples', 'brick')), parts along dimension 0, may hold values from -6 to 6
- log_perm: float32 [128, 128, 256], P(('samples', 'brick')), parts along dimension 0, may hold values from -3 to 3
- owner: int32 [16], replicated, may hold values from 0 to 15, each once
Outputs:
- corrected: float32 [128, 128, 256], P(('samples', 'brick')), parts along dimension 0
- coarse_held: float32 [32, 2048], P(('samples', 'brick')), parts along dimension 0
There are 2 independent parts, one for each index of `samples`. A program takes and returns all parts, laid end to end along the dimension named above; an argument that names none is the same for every part. Nothing has to cross between parts.
Inputs may be any that keep to these rules, and one draw needn't show every extreme that they name: `owner`: each brick index appears exactly once.
All inputs are finite; a program needn't handle non-finite values.
Results may differ from a plain program's by a relative error of at most 0.00005.
Values sent between devices are 32-bit elements; how exact they have to be, the bound alone decides.
A program may use at most 64 MiB of HBM per device.

v0:
```python
import functools

import jax
import jax.numpy as jnp
import ml_dtypes
import numpy as np
from jax import lax
from jax.experimental import pallas as pl
from jax.experimental.pallas import tpu as pltpu
from jax.sharding import PartitionSpec as P

SWEEPS = 8
CHUNKS = 8
MESH = pl.DeviceIdType.MESH
F32 = jnp.float32
BF16 = jnp.bfloat16


def prolong_matrix(n_fine):
    i = np.arange(n_fine)[:, None]
    j = np.arange(n_fine // 4)[None, :]
    base, offset = i // 4, i % 4
    own = np.where((offset == 0) | (offset == 3), 0.625, 0.875)
    side = np.where(offset < 2, -1, 1)
    return np.where(j == base, own, 0.0) + np.where(j == base + side, 1.0 - own, 0.0)


def mean_matrix(n_fine):
    i = np.arange(n_fine)[:, None]
    j = np.arange(n_fine // 4)[None, :]
    return np.where(j == i // 4, 1.0, 0.0)


def even_odd(m):
    return np.concatenate([m[:, 0::2], m[:, 1::2]], axis=1)


def halves(m):
    zero = np.zeros_like(m)
    return np.stack([np.concatenate([m, zero], 1), np.concatenate([zero, m], 1)])


def split(x):
    hi = x.astype(BF16)
    return hi, (x - hi.astype(F32)).astype(BF16)


def dot(a, b):
    return jnp.dot(a, b, preferred_element_type=F32)


def to_coarse(y_mat, z_mat, x):
    hi, lo = split(x)
    a = dot(y_mat, hi) + dot(y_mat, lo)
    hi, lo = split(a)
    h = a.shape[0] // 2
    return (
        dot(hi[:h], z_mat[0]) + dot(lo[:h], z_mat[0]) + dot(hi[h:], z_mat[1]) + dot(lo[h:], z_mat[1])
    )


def smooth_kernel(
    n, ny, nz,
    source_hbm, guess_hbm, logq_hbm, ry_hbm, rz_hbm, my_hbm, mz_hbm,
    smooth_hbm, all_rhs, coef_hbm, scaled_hbm,
    coef, scaled, ry, rz, my, mz, all_q, q_pad, src, logq, K, U0, U1, U2, D, N, EK, X, H, own, part,
    local_sem, halo_send, halo_recv, part_send, part_recv, q_send, q_recv, r_send, r_recv,
):
    me = lax.axis_index("brick")
    R = ny // CHUNKS
    has = (me > 0, me < n - 1)
    peer_of = (me - 1, me + 1)

    loads = [
        pltpu.make_async_copy(logq_hbm, logq, local_sem.at[0]),
        pltpu.make_async_copy(guess_hbm, U0.at[pl.ds(1, 4), pl.ds(8, ny)], local_sem.at[1]),
        pltpu.make_async_copy(source_hbm, src, local_sem.at[2]),
        pltpu.make_async_copy(my_hbm, my, local_sem.at[3]),
        pltpu.make_async_copy(mz_hbm, mz, local_sem.at[4]),
        pltpu.make_async_copy(ry_hbm, ry, local_sem.at[5]),
        pltpu.make_async_copy(rz_hbm, rz, local_sem.at[6]),
    ]
    for copy in loads:
        copy.start()

    barrier = pltpu.get_barrier_semaphore()

    def greet(k, _):
        pl.semaphore_signal(
            barrier, inc=1, device_id={"brick": lax.rem(me + k, n)}, device_id_type=MESH
        )
        return 0

    lax.fori_loop(1, n, greet, 0)
    pl.semaphore_wait(barrier, n - 1)

    def halo(which, side, c):
        plane = 3 * side
        start = c * R if isinstance(c, int) else pl.multiple_of(c * R, R)
        rows = pl.ds(start, R)
        if which == 2:
            ref = U1.at[plane + 1, pl.ds(start + 8, R)]
        else:
            ref = (logq_hbm, guess_hbm)[which].at[plane, rows]
        return pltpu.make_async_remote_copy(
            src_ref=ref,
            dst_ref=H.at[which, 1 - side, rows],
            send_sem=halo_send.at[which, side, c],
            recv_sem=halo_recv.at[which, 1 - side, c],
            device_id={"brick": peer_of[side]},
            device_id_type=MESH,
        )

    def arrival(which, side, c):
        start = c * R if isinstance(c, int) else pl.multiple_of(c * R, R)
        ref = H.at[which, side, pl.ds(start, R)]
        return pltpu.make_async_remote_copy(
            src_ref=ref,
            dst_ref=ref,
            send_sem=halo_send.at[which, side, c],
            recv_sem=halo_recv.at[which, side, c],
            device_id={"brick": peer_of[side]},
            device_id_type=MESH,
        )

    for c in range(CHUNKS):
        for side in range(2):

            @pl.when(has[side])
            def _():
                halo(0, side, c).start()
                halo(1, side, c).start()

    zero_plane = jnp.zeros((ny + 16, nz), F32)
    zero_rows = jnp.zeros((8, nz), F32)
    for ref in (K, U0, U1, U2):
        ref[0] = zero_plane
        ref[5] = zero_plane
        for p in range(1, 5):
            ref[p, 0:8] = zero_rows
            ref[p, ny + 8 : ny + 16] = zero_rows

    lane = lax.broadcasted_iota(jnp.int32, (R, nz), 1)
    first, last = lane == 0, lane == nz - 1

    def yz(window):
        center = window[8 : R + 8]
        low = jnp.where(first, 0.0, pltpu.roll(center, 1, 1))
        high = jnp.where(last, 0.0, pltpu.roll(center, nz - 1, 1))
        return (window[7 : R + 7] + window[9 : R + 9]) + (low + high)

    loads[0].wait()

    def exps(i, _):
        p, start = i // CHUNKS, pl.multiple_of((i % CHUNKS) * R, R)
        K[p + 1, pl.ds(start + 8, R)] = jnp.exp(logq[p, pl.ds(start, R)])
        return 0

    lax.fori_loop(0, 4 * CHUNKS, exps, 0)
    for copy in loads[1:]:
        copy.wait()

    def nearby(U, p, start):
        at = pl.ds(start + 8, R)
        window = pl.ds(start, R + 16)
        u, k = U[p + 1, window], K[p + 1, window]
        um, up, km, kp = U[p, at], U[p + 2, at], K[p, at], K[p + 2, at]
        su = yz(u) + (um + up)
        sku = yz(u * k) + (km * um + kp * up)
        q = k[8 : R + 8]
        return u[8 : R + 8], q, k, km + kp, 0.5 * (q * su + sku)

    def sweep_one(i, _):
        p, start = i // CHUNKS, pl.multiple_of((i % CHUNKS) * R, R)
        rows = pl.ds(start, R)
        u, q, k, kx, near = nearby(U0, p, start)
        d = 3.0 * q + 0.5 * (yz(k) + kx)
        total = src[p, rows] + near
        D[p, rows] = d
        N[p, rows] = total
        U1[p + 1, pl.ds(start + 8, R)] = 0.2 * u + 0.8 * total / d
        return 0

    lax.fori_loop(0, 4 * CHUNKS, sweep_one, 0)

    own[...] = to_coarse(
        my[...], mz, (K[1, 8 : ny + 8] + K[2, 8 : ny + 8]) + (K[3, 8 : ny + 8] + K[4, 8 : ny + 8])
    ) * (1.0 / 64.0)
    all_q[me] = own[...]

    def finish_one(c, _):
        start = pl.multiple_of(c * R, R)
        rows, at = pl.ds(start, R), pl.ds(start + 8, R)
        for side in range(2):
            p = 3 * side

            @pl.when(has[side])
            def _():
                arrival(0, side, c).wait_recv()
                arrival(1, side, c).wait_recv()
                q = K[p + 1, at]
                kh = jnp.exp(H[0, side, rows])
                EK[side, rows] = kh
                D[p, rows] = D[p, rows] + 0.5 * kh
                N[p, rows] = N[p, rows] + 0.5 * (q + kh) * H[1, side, rows]

            @pl.when(jnp.logical_not(has[side]))
            def _():
                EK[side, rows] = jnp.zeros((R, nz), F32)

            U1[p + 1, at] = 0.2 * U0[p + 1, at] + 0.8 * N[p, rows] / D[p, rows]

            @pl.when(has[side])
            def _():
                halo(2, side, c).start()

        return 0

    def spread(block, ref, k, send, recv):
        return pltpu.make_async_remote_copy(
            src_ref=block,
            dst_ref=ref.at[me],
            send_sem=send.at[k],
            recv_sem=recv.at[me],
            device_id={"brick": lax.rem(me + k, n)},
            device_id_type=MESH,
        )

    def landed(ref, k, send, recv):
        who = lax.rem(me + k, n)
        return pltpu.make_async_remote_copy(
            src_ref=ref.at[who],
            dst_ref=ref.at[who],
            send_sem=send.at[k],
            recv_sem=recv.at[who],
            device_id={"brick": who},
            device_id_type=MESH,
        )

    def send_q(k, _):
        spread(all_q.at[me], all_q, k, q_send, q_recv).start()
        return 0

    def sweep_two(p, start):
        rows = pl.ds(start, R)
        u, q, k, kx, near = nearby(U1, p, start)
        total = src[p, rows] + near
        N[p, rows] = total
        U2[p + 1, pl.ds(start + 8, R)] = 0.2 * u + 0.8 * total / D[p, rows]
        return 0

    def first_stage(c, _):
        @pl.when(c < CHUNKS)
        def _():
            finish_one(c, 0)

        @pl.when(c == CHUNKS - 1)
        def _():
            lax.fori_loop(1, n, send_q, 0)

        @pl.when(c > 0)
        def _():
            start = pl.multiple_of((c - 1) * R, R)
            lax.fori_loop(0, 4, lambda p, _: sweep_two(p, start), 0)

        return 0

    lax.fori_loop(0, CHUNKS + 1, first_stage, 0)

    def finish_two(c, _):
        start = pl.multiple_of(c * R, R)
        rows, at = pl.ds(start, R), pl.ds(start + 8, R)
        for side in range(2):
            p = 3 * side

            @pl.when(has[side])
            def _():
                arrival(2, side, c).wait_recv()
                total = N[p, rows] + 0.5 * (K[p + 1, at] + EK[side, rows]) * H[2, side, rows]
                U2[p + 1, at] = 0.2 * U1[p + 1, at] + 0.8 * total / D[p, rows]

        return 0

    present = [jnp.where(flag, 0.5, 0.0).astype(F32) for flag in has]

    def residual(c, _):
        start = pl.multiple_of(c * R, R)
        rows, at = pl.ds(start, R), pl.ds(start + 8, R)

        def row(p):
            u, q, k, kx, near = nearby(U2, p, start)
            return src[p, rows] - D[p, rows] * u + near

        r0, r1 = row(0), row(1)
        flo = present[0] * (K[1, at] + EK[0, rows]) * U2[1, at]
        X[0, rows] = 0.625 * flo + 0.375 * r0 + 0.125 * r1
        X[1, rows] = 0.375 * flo + 0.625 * r0 + 0.875 * r1
        r2, r3 = row(2), row(3)
        fhi = present[1] * (K[4, at] + EK[1, rows]) * U2[4, at]
        X[2, rows] = 0.625 * fhi + 0.375 * r3 + 0.125 * r2
        X[1, rows] = X[1, rows] + (0.375 * fhi + 0.625 * r3 + 0.875 * r2)
        return 0

    def second_stage(c, _):
        @pl.when(c < CHUNKS)
        def _():
            finish_two(c, 0)

        @pl.when(c > 0)
        def _():
            residual(c - 1, 0)

        return 0

    lax.fori_loop(0, CHUNKS + 1, second_stage, 0)

    stores = [
        pltpu.make_async_copy(U2.at[pl.ds(1, 4), pl.ds(8, ny)], smooth_hbm, local_sem.at[0]),
        pltpu.make_async_copy(own, all_rhs.at[me], local_sem.at[1]),
        pltpu.make_async_copy(coef, coef_hbm, local_sem.at[2]),
        pltpu.make_async_copy(scaled, scaled_hbm, local_sem.at[3]),
    ]
    stores[0].start()

    def partial(side):
        return pltpu.make_async_remote_copy(
            src_ref=part.at[side],
            dst_ref=part.at[3 - side],
            send_sem=part_send.at[side],
            recv_sem=part_recv.at[1 - side],
            device_id={"brick": peer_of[side]},
            device_id_type=MESH,
        )

    def partial_in(side):
        return pltpu.make_async_remote_copy(
            src_ref=part.at[2 + side],
            dst_ref=part.at[2 + side],
            send_sem=part_send.at[side],
            recv_sem=part_recv.at[side],
            device_id={"brick": peer_of[side]},
            device_id_type=MESH,
        )

    for side in range(2):
        part[side] = to_coarse(ry[...], rz, X[2 * side])

    for side in range(2):

        @pl.when(has[side])
        def _():
            partial(side).start()

    own[...] = to_coarse(ry[...], rz, X[1])
    for side in range(2):

        @pl.when(has[side])
        def _():
            partial_in(side).wait_recv()
            own[...] = own[...] + part[2 + side]

    own[...] = own[...] * (1.0 / 64.0)
    stores[1].start()

    def send_r(k, _):
        spread(own, all_rhs, k, r_send, r_recv).start()
        return 0

    lax.fori_loop(1, n, send_r, 0)

    def settle_q(k, _):
        landed(all_q, k, q_send, q_recv).wait_recv()
        spread(all_q.at[me], all_q, k, q_send, q_recv).wait_send()
        return 0

    def settle_r(k, _):
        landed(all_rhs, k, r_send, r_recv).wait_recv()
        spread(own, all_rhs, k, r_send, r_recv).wait_send()
        return 0

    lax.fori_loop(1, n, settle_q, 0)
    coarse_coefficients(n, min(8, n), all_q, q_pad, coef, scaled)
    stores[2].start()
    stores[3].start()

    for side in range(2):

        @pl.when(has[side])
        def _():
            for c in range(CHUNKS):
                for which in range(3):
                    halo(which, side, c).wait_send()
            partial(side).wait_send()

    lax.fori_loop(1, n, settle_r, 0)
    for copy in stores:
        copy.wait()


def coarse_shifts(shape):
    rows, lanes = shape[1:]
    cz = lanes // 2
    row = lax.broadcasted_iota(jnp.int32, shape, 1)
    lane = lax.broadcasted_iota(jnp.int32, shape, 2)
    low_half = lane < cz
    z = jnp.where(low_half, lane, lane - cz)
    outside = (
        (row == 0) & low_half,
        (row == rows - 1) & jnp.logical_not(low_half),
        z == 0,
        z == cz - 1,
    )

    def shifts(c):
        swapped = pltpu.roll(c, cz, 2)
        y_low = jnp.where(low_half, pltpu.roll(swapped, 1, 1), swapped)
        y_high = jnp.where(low_half, swapped, pltpu.roll(swapped, rows - 1, 1))
        return y_low, y_high, pltpu.roll(c, 1, 2), pltpu.roll(c, lanes - 1, 2)

    return shifts, outside


def coarse_coefficients(n, group, perm, q_pad, coef, scaled):
    rows, lanes = perm.shape[1:]
    shifts, outside = coarse_shifts((group, rows, lanes))
    edge = jnp.zeros((rows, lanes), F32)
    q_pad[0] = edge
    q_pad[n + 1] = edge
    q_pad[1 : n + 1] = perm[...]

    def prepare(g, _):
        at = pl.multiple_of(g * group, group)
        q = q_pad[pl.ds(at + 1, group)]
        near = [q_pad[pl.ds(at, group)], q_pad[pl.ds(at + 2, group)]]
        near += [jnp.where(out, 0.0, v) for out, v in zip(outside, shifts(q))]
        faces = [0.5 * (q + v) for v in near]
        diagonal = ((faces[0] + faces[1]) + (faces[2] + faces[3])) + (faces[4] + faces[5])
        scale = 0.8 / diagonal
        for k, out in enumerate((None, None) + outside):
            f = faces[k] * scale
            coef[k, pl.ds(at, group)] = f if out is None else jnp.where(out, 0.0, f)
        scaled[pl.ds(at, group)] = 16.0 * scale
        return 0

    lax.fori_loop(0, n // group, prepare, 0)


def coarse_kernel(
    n, group,
    owner_hbm, rhs_hbm, coef_hbm, scaled_hbm, smooth_hbm, ez_hbm, ey_hbm,
    corrected_hbm, held,
    owner, rhs, coef, scaled, smooth, ez, ey, C, B, corrected, sem,
):
    me = lax.axis_index("brick")
    loads = [
        pltpu.make_async_copy(*pair, sem.at[4 + k])
        for k, pair in enumerate(
            (
                (rhs_hbm, rhs), (scaled_hbm, scaled), (coef_hbm, coef),
                (ez_hbm, ez), (ey_hbm, ey), (smooth_hbm, smooth), (owner_hbm, owner),
            )
        )
    ]
    for load in loads:
        load.start()
    rows, lanes = rhs.shape[1:]
    shifts, _ = coarse_shifts((group, rows, lanes))
    edge = jnp.zeros((rows, lanes), F32)
    for slot in range(2):
        C[slot, 0] = edge
        C[slot, n + 1] = edge
    loads[0].wait()
    loads[1].wait()
    B[...] = rhs[...] * scaled[...]
    C[0, 1 : n + 1] = B[...]

    loads[2].wait()
    for sweep in range(SWEEPS - 1):
        now, later = sweep % 2, 1 - sweep % 2

        def step(g, _):
            at = pl.multiple_of(g * group, group)
            c = C[now, pl.ds(at + 1, group)]
            near = (C[now, pl.ds(at, group)], C[now, pl.ds(at + 2, group)]) + shifts(c)
            terms = [coef[k, pl.ds(at, group)] * v for k, v in enumerate(near)]
            total = B[pl.ds(at, group)] + 0.2 * c
            total = (total + (terms[0] + terms[1])) + ((terms[2] + terms[3]) + (terms[4] + terms[5]))
            C[later, pl.ds(at + 1, group)] = total
            return 0

        lax.fori_loop(0, n // group, step, 0)

    final = (SWEEPS - 1) % 2

    for load in loads[3:]:
        load.wait()
    below, mid, above = C[final, me], C[final, me + 1], C[final, me + 2]
    planes = jnp.concatenate(
        [
            0.625 * mid + 0.375 * below,
            0.875 * mid + 0.125 * below,
            0.875 * mid + 0.125 * above,
            0.625 * mid + 0.375 * above,
        ],
        axis=0,
    )
    hi, lo = split(planes)
    even = dot(hi, ez[0]) + dot(lo, ez[0])
    odd = dot(hi, ez[1]) + dot(lo, ez[1])
    for p in range(4):
        both = jnp.concatenate(
            [even[p * rows : (p + 1) * rows], odd[p * rows : (p + 1) * rows]], axis=0
        )
        hi, lo = split(both)
        corrected[p] = smooth[p] + (dot(ey[...], hi) + dot(ey[...], lo))
        pltpu.make_async_copy(corrected.at[p], corrected_hbm.at[p], sem.at[p]).start()

    mine = jnp.zeros((rows, lanes), F32)
    for b in range(n):
        mine = jnp.where(owner[b] == me, C[final, b + 1], mine)
    for r in range(rows):
        held[0:1, r * lanes : (r + 1) * lanes] = mine[r : r + 1]
    for p in range(4):
        pltpu.make_async_copy(corrected.at[p], corrected_hbm.at[p], sem.at[p]).wait()


def local(n, source, guess, log_perm, owner):
    planes, ny, nz = source.shape
    assert planes == 4
    cells = (ny // 4) * (nz // 4)
    rows, lanes = ny // 8, nz // 2
    dense = (rows, lanes)
    as_bf16 = lambda m: jnp.asarray(m.astype(ml_dtypes.bfloat16))
    py, pz = even_odd(prolong_matrix(ny)), prolong_matrix(nz)
    ry, rz = as_bf16(py.T), as_bf16(halves(pz))
    my, mz = as_bf16(even_odd(mean_matrix(ny)).T), as_bf16(halves(mean_matrix(nz)))
    ey, ez = as_bf16(py), as_bf16(halves(pz).transpose(0, 2, 1))
    vmem = pl.BlockSpec(memory_space=pltpu.VMEM)
    hbm = pl.BlockSpec(memory_space=pl.ANY)
    whole = lambda *s: pltpu.VMEM(s, F32)
    dma = lambda *s: pltpu.SemaphoreType.DMA(s)
    padded = (6, ny + 16, nz)
    smooth, all_rhs, coef, scaled = pl.pallas_call(
        functools.partial(smooth_kernel, n, ny, nz),
        out_shape=(
            jax.ShapeDtypeStruct((4, ny, nz), F32),
            jax.ShapeDtypeStruct((n,) + dense, F32),
            jax.ShapeDtypeStruct((6, n) + dense, F32),
            jax.ShapeDtypeStruct((n,) + dense, F32),
        ),
        in_specs=[hbm] * 7,
        out_specs=(hbm,) * 4,
        scratch_shapes=[
            whole(6, n, *dense), whole(n, *dense),
            pltpu.VMEM(ry.shape, BF16), pltpu.VMEM(rz.shape, BF16),
            pltpu.VMEM(my.shape, BF16), pltpu.VMEM(mz.shape, BF16),
            whole(n, *dense), whole(n + 2, *dense),
            whole(4, ny, nz), whole(4, ny, nz),
            whole(*padded), whole(*padded), whole(*padded), whole(*padded),
            whole(4, ny, nz), whole(4, ny, nz),
            whole(2, ny, nz), whole(3, ny, nz), whole(3, 2, ny, nz),
            whole(*dense), whole(4, *dense),
            dma(7), dma(3, 2, CHUNKS), dma(3, 2, CHUNKS), dma(2), dma(2),
            dma(n), dma(n), dma(n), dma(n),
        ],
        compiler_params=pltpu.CompilerParams(
            collective_id=0, has_side_effects=True, vmem_limit_bytes=60 * 2**20
        ),
        name="smooth",
    )(source, guess, log_perm, ry, rz, my, mz)
    return pl.pallas_call(
        functools.partial(coarse_kernel, n, min(16, n)),
        out_shape=(
            jax.ShapeDtypeStruct((4, ny, nz), F32),
            jax.ShapeDtypeStruct((1, cells), F32),
        ),
        in_specs=[hbm] * 7,
        out_specs=(hbm, vmem),
        scratch_shapes=[
            pltpu.SMEM((n,), jnp.int32),
            whole(n, *dense), whole(6, n, *dense), whole(n, *dense), whole(4, ny, nz),
            pltpu.VMEM(ez.shape, BF16), pltpu.VMEM(ey.shape, BF16),
            whole(2, n + 2, *dense), whole(n, *dense), whole(4, ny, nz), dma(11),
        ],
        compiler_params=pltpu.CompilerParams(vmem_limit_bytes=60 * 2**20),
        name="coarse",
    )(owner, all_rhs, coef, scaled, smooth, ez, ey)


def solution(mesh):
    spec = P(("samples", "brick"), None, None)
    return jax.shard_map(
        functools.partial(local, mesh.shape["brick"]),
        mesh=mesh,
        in_specs=(spec, spec, spec, P()),
        out_specs=(spec, P(("samples", "brick"), None)),
        check_vma=False,
    )
```

profile of v0, /device:TPU:1, one launch (start us, length us, event | category | flops | bytes accessed | tf_op | source)
XLA Modules:
  0.0 30.0 jit_solution(9451257044342322843)
XLA Ops:
  0.6 25.2 %smooth.1 = (f32[4,128,256]{2,1,0:T(8,128)}, f32[16,16,128]{2,1,0:T(8,128)}, f32[6,16,16,128]{3,2,1,0:T(8,128)}, f32[16,16,128]{2,1,0:T(8,128)}) custom-call(f32[4,128,256]{2,1,0:T(8,128)} %source_hbm.1, f32[4,128,256]{2,1,0:T(8,128)} %guess_hbm.1, f32[4,128,256]{2,1,0:T(8,128)} %logq_hbm.1, bf16[32,128]{1,0:T(8,128)(2,1)} %constant.12.clone.ry_hbm, ...), custom_call_target="tpu_custom_call" | custom-call | tf_op jit(solution)/shard_map/smooth/pallas_call | solution.py:543
  25.8 4.2 %coarse.1 = (f32[4,128,256]{2,1,0:T(8,128)}, f32[1,2048]{1,0:T(1,128)}) custom-call(s32[16]{0:T(128)} %owner_hbm.1, f32[16,16,128]{2,1,0:T(8,128)} %get-tuple-element.6.rhs_hbm, f32[6,16,16,128]{3,2,1,0:T(8,128)} %get-tuple-element.7.coef_hbm, f32[16,16,128]{2,1,0:T(8,128)} %get-tuple-element.8.scaled_hbm, f32[4,128,256]{2,1,0:T(8,128)} %get-tuple-element.9.smooth_hbm, ...), custom_call_target="tpu_custom_call" | custom-call | tf_op jit(solution)/shard_map/coarse/pallas_call | solution.py:571
where the time goes:
time: 30.5 us; the launch traced here: 30 us
  Pallas kernels  29.3 us (96%)
  between operations  0.64 us (2%)
    pallas_call x1, Pallas kernels, local(): pl.pallas_call(functools.partial(smooth_kernel, n, ny, nz), out_shape=(ja...  25.2 us
    pallas_call x1, Pallas kernels, local(): pl.pallas_call(functools.partial(coarse_kernel, n, min(16, n)), out_shape...  4.18 us

commit v1 on v0

v1 whole, which is shorter than its diff:
```python
import functools

import jax
import jax.numpy as jnp
import ml_dtypes
import numpy as np
from jax import lax
from jax.experimental import pallas as pl
from jax.experimental.pallas import tpu as pltpu
from jax.sharding import PartitionSpec as P

SWEEPS = 8
CHUNKS = 8
MESH = pl.DeviceIdType.MESH
F32 = jnp.float32
BF16 = jnp.bfloat16


def prolong_matrix(n_fine):
    i = np.arange(n_fine)[:, None]
    j = np.arange(n_fine // 4)[None, :]
    base, offset = i // 4, i % 4
    own = np.where((offset == 0) | (offset == 3), 0.625, 0.875)
    side = np.where(offset < 2, -1, 1)
    return np.where(j == base, own, 0.0) + np.where(j == base + side, 1.0 - own, 0.0)


def mean_matrix(n_fine):
    i = np.arange(n_fine)[:, None]
    j = np.arange(n_fine // 4)[None, :]
    return np.where(j == i // 4, 1.0, 0.0)


def even_odd(m):
    return np.concatenate([m[:, 0::2], m[:, 1::2]], axis=1)


def halves(m):
    zero = np.zeros_like(m)
    return np.stack([np.concatenate([m, zero], 1), np.concatenate([zero, m], 1)])


def split(x):
    hi = x.astype(BF16)
    return hi, (x - hi.astype(F32)).astype(BF16)


def dot(a, b):
    return jnp.dot(a, b, preferred_element_type=F32)


def to_coarse(y_mat, z_mat, x):
    hi, lo = split(x)
    a = dot(y_mat, hi) + dot(y_mat, lo)
    hi, lo = split(a)
    h = a.shape[0] // 2
    return (
        dot(hi[:h], z_mat[0]) + dot(lo[:h], z_mat[0]) + dot(hi[h:], z_mat[1]) + dot(lo[h:], z_mat[1])
    )


def smooth_kernel(
    n, ny, nz, group,
    source_hbm, guess_hbm, logq_hbm, owner_hbm, ry_hbm, rz_hbm, my_hbm, mz_hbm, ez_hbm, ey_hbm,
    U2, C, ez, ey, holder,
    owner, coef, scaled, ry, rz, my, mz, all_q, q_pad, all_r, B, src, logq, K, U0, U1, D, W, N, F, X, H, part,
    local_sem, halo_send, halo_recv, part_send, part_recv, q_send, q_recv, r_send, r_recv, token_sem,
):
    me = lax.axis_index("brick")
    R = ny // CHUNKS
    half = n // 2
    has = (me > 0, me < n - 1)
    flag = [jnp.where(h, 1.0, 0.0).astype(F32) for h in has]
    peer_of = (me - 1, me + 1)
    sibling = me + 1 - 2 * lax.rem(me, 2)

    loads = [
        pltpu.make_async_copy(logq_hbm, logq, local_sem.at[0]),
        pltpu.make_async_copy(guess_hbm, U0.at[:, pl.ds(8, ny)], local_sem.at[1]),
        pltpu.make_async_copy(source_hbm, src, local_sem.at[2]),
        pltpu.make_async_copy(my_hbm, my, local_sem.at[3]),
        pltpu.make_async_copy(mz_hbm, mz, local_sem.at[4]),
        pltpu.make_async_copy(ry_hbm, ry, local_sem.at[5]),
        pltpu.make_async_copy(rz_hbm, rz, local_sem.at[6]),
        pltpu.make_async_copy(ez_hbm, ez, local_sem.at[7]),
        pltpu.make_async_copy(ey_hbm, ey, local_sem.at[8]),
        pltpu.make_async_copy(owner_hbm, owner, local_sem.at[9]),
    ]

    def signal(sem, who):
        pl.semaphore_signal(sem, inc=1, device_id={"brick": who}, device_id_type=MESH)

    barrier = pltpu.get_barrier_semaphore()

    def greet(sem, distance):
        @pl.when(me >= distance)
        def _():
            signal(sem, me - distance)

        @pl.when(me + distance < n)
        def _():
            signal(sem, me + distance)

    def greeted(sem, distance):
        low = jnp.where(me >= distance, 1, 0)
        high = jnp.where(me + distance < n, 1, 0)
        pl.semaphore_wait(sem, low + high)

    distances = [2**k for k in range((n - 1).bit_length())]

    greet(barrier, 1)
    for copy in loads:
        copy.start()

    zero_rows = jnp.zeros((8, nz), F32)
    for ref in (K, U0, U1, U2):
        for p in range(4):
            ref[p, 0:8] = zero_rows
            ref[p, ny + 8 : ny + 16] = zero_rows
    for side in range(2):

        @pl.when(jnp.logical_not(has[side]))
        def _():
            for which in range(3):
                H[which, side] = jnp.zeros((ny, nz), F32)

    greeted(barrier, 1)

    def rows_at(c):
        return pl.ds(c * R if isinstance(c, int) else pl.multiple_of(c * R, R), R)

    def rows_in(c):
        return pl.ds(8 + c * R if isinstance(c, int) else pl.multiple_of(c * R, R) + 8, R)

    def halo(which, side, c):
        plane = 3 * side
        if which == 2:
            ref = U1.at[plane, rows_in(c)]
        else:
            ref = (logq_hbm, guess_hbm)[which].at[plane, rows_at(c)]
        return pltpu.make_async_remote_copy(
            src_ref=ref,
            dst_ref=H.at[which, 1 - side, rows_at(c)],
            send_sem=halo_send.at[which, side, c],
            recv_sem=halo_recv.at[which, 1 - side, c],
            device_id={"brick": peer_of[side]},
            device_id_type=MESH,
        )

    def arrival(which, side, c):
        ref = H.at[which, side, rows_at(c)]
        return pltpu.make_async_remote_copy(
            src_ref=ref,
            dst_ref=ref,
            send_sem=halo_send.at[which, side, c],
            recv_sem=halo_recv.at[which, side, c],
            device_id={"brick": peer_of[side]},
            device_id_type=MESH,
        )

    for c in range(CHUNKS):
        for side in range(2):

            @pl.when(has[side])
            def _():
                halo(0, side, c).start()
                halo(1, side, c).start()

    greet(token_sem.at[0], 1)

    lane = lax.broadcasted_iota(jnp.int32, (R, nz), 1)
    first, last = lane == 0, lane == nz - 1

    def middle(window):
        return window[8 : R + 8]

    def yz(window):
        center = middle(window)
        low = jnp.where(first, 0.0, pltpu.roll(center, 1, 1))
        high = jnp.where(last, 0.0, pltpu.roll(center, nz - 1, 1))
        return (window[7 : R + 7] + window[9 : R + 9]) + (low + high)

    def across(windows, p):
        total = yz(windows[p])
        if p > 0:
            total = total + middle(windows[p - 1])
        if p < 3:
            total = total + middle(windows[p + 1])
        return total

    loads[0].wait()

    def exps(c, _):
        for p in range(4):
            K[p, rows_in(c)] = jnp.exp(logq[p, rows_at(c)])
        return 0

    lax.fori_loop(0, CHUNKS, exps, 0)
    for copy in loads[1:]:
        copy.wait()

    def windows(ref, c):
        at = pl.ds(pl.multiple_of(c * R, R), R + 16)
        return [ref[p, at] for p in range(4)]

    def nearby(u, k):
        uk = [a * b for a, b in zip(u, k)]
        return [0.5 * (middle(k[p]) * across(u, p) + across(uk, p)) for p in range(4)]

    def sweep_one(c, _):
        rows, at = rows_at(c), rows_in(c)
        u, k = windows(U0, c), windows(K, c)
        near = nearby(u, k)
        for p in range(4):
            d = 3.0 * middle(k[p]) + 0.5 * across(k, p)
            total = src[p, rows] + near[p]
            D[p, rows] = d
            if p in (0, 3):
                N[p, rows] = total
            else:
                w = 0.8 / d
                W[p, rows] = w
                U1[p, at] = 0.2 * middle(u[p]) + w * total
        return 0

    lax.fori_loop(0, CHUNKS, sweep_one, 0)
    greeted(token_sem.at[0], 1)

    all_q[me] = to_coarse(
        my[...], mz, (K[0, 8 : ny + 8] + K[1, 8 : ny + 8]) + (K[2, 8 : ny + 8] + K[3, 8 : ny + 8])
    ) * (1.0 / 64.0)
    for b in range(n):
        holder[b : b + 1] = jnp.full((1, 128), owner[b], jnp.int32)

    for k in range(1, len(distances)):
        greet(token_sem.at[k], distances[k])
        if k + 1 < len(distances):
            greeted(token_sem.at[k], distances[k])

    def finish_one(c):
        rows, at = rows_at(c), rows_in(c)
        for side in range(2):

            @pl.when(has[side])
            def _():
                arrival(0, side, c).wait_recv()
                arrival(1, side, c).wait_recv()

        for side in range(2):
            p = 3 * side
            kh = jnp.exp(H[0, side, rows]) * flag[side]
            face = 0.5 * (K[p, at] + kh)
            d = D[p, rows] + 0.5 * kh
            w = 0.8 / d
            F[side, rows] = face
            D[p, rows] = d
            W[p, rows] = w
            U1[p, at] = 0.2 * U0[p, at] + w * (N[p, rows] + face * H[1, side, rows])
        for side in range(2):

            @pl.when(has[side])
            def _():
                halo(2, side, c).start()

    def copy_to(ref, slot, who, send, recv):
        return pltpu.make_async_remote_copy(
            src_ref=ref.at[slot],
            dst_ref=ref.at[slot],
            send_sem=send,
            recv_sem=recv.at[slot],
            device_id={"brick": who},
            device_id_type=MESH,
        )

    def direct(ref, j, send, recv):
        return copy_to(ref, me, lax.rem(me + 2 * j, n), send.at[j], recv)

    def handed(ref, j, send, recv):
        who = lax.rem(me + n - 2 * j, n)
        return copy_to(ref, who, sibling, send.at[half + j], recv)

    def to_sibling(ref, send, recv):
        return copy_to(ref, me, sibling, send.at[0], recv)

    def spread(ref, send, recv):
        def body(j, _):
            direct(ref, j, send, recv).start()
            return 0

        lax.fori_loop(1, half, body, 0)
        to_sibling(ref, send, recv).start()

    def hand_on(ref, send, recv):
        def body(j, _):
            copy = handed(ref, j, send, recv)
            copy.wait_recv()
            copy.start()
            return 0

        lax.fori_loop(1, half, body, 0)

    def collect(ref, send, recv):
        def body(j, _):
            slot = lax.rem(sibling + n - 2 * j, n)
            copy_to(ref, slot, sibling, send.at[half + j], recv).wait_recv()
            return 0

        lax.fori_loop(0, half, body, 0)

    def sent(ref, send, recv):
        def body(j, _):
            direct(ref, j, send, recv).wait_send()
            handed(ref, j, send, recv).wait_send()
            return 0

        lax.fori_loop(1, half, body, 0)
        to_sibling(ref, send, recv).wait_send()

    def sweep_two(c):
        rows, at = rows_at(c), rows_in(c)
        u = windows(U1, c)
        near = nearby(u, windows(K, c))
        for p in range(4):
            total = src[p, rows] + near[p]
            if p in (0, 3):
                N[p, rows] = total
            else:
                U2[p, at] = 0.2 * middle(u[p]) + W[p, rows] * total

    def first_stage(c, _):
        @pl.when(c < CHUNKS)
        def _():
            finish_one(c)

        @pl.when(c == CHUNKS - 1)
        def _():
            greeted(token_sem.at[len(distances) - 1], distances[-1])
            spread(all_q, q_send, q_recv)

        @pl.when(c > 0)
        def _():
            sweep_two(c - 1)

        return 0

    lax.fori_loop(0, CHUNKS + 1, first_stage, 0)

    def finish_two(c):
        rows, at = rows_at(c), rows_in(c)
        for side in range(2):

            @pl.when(has[side])
            def _():
                arrival(2, side, c).wait_recv()

        for side in range(2):
            p = 3 * side
            total = N[p, rows] + F[side, rows] * H[2, side, rows]
            U2[p, at] = 0.2 * U1[p, at] + W[p, rows] * total

    def residual(c):
        rows = rows_at(c)
        u = windows(U2, c)
        near = nearby(u, windows(K, c))
        r = [src[p, rows] - D[p, rows] * middle(u[p]) + near[p] for p in range(4)]
        flo = flag[0] * F[0, rows] * middle(u[0])
        fhi = flag[1] * F[1, rows] * middle(u[3])
        X[0, rows] = 0.625 * flo + 0.375 * r[0] + 0.125 * r[1]
        X[1, rows] = (0.375 * flo + 0.625 * r[0] + 0.875 * r[1]) + (0.375 * fhi + 0.625 * r[3] + 0.875 * r[2])
        X[2, rows] = 0.625 * fhi + 0.375 * r[3] + 0.125 * r[2]

    def second_stage(c, _):
        @pl.when(c < CHUNKS)
        def _():
            finish_two(c)

        @pl.when(c > 0)
        def _():
            residual(c - 1)

        return 0

    lax.fori_loop(0, CHUNKS + 1, second_stage, 0)

    def partial(side):
        return pltpu.make_async_remote_copy(
            src_ref=part.at[side],
            dst_ref=part.at[3 - side],
            send_sem=part_send.at[side],
            recv_sem=part_recv.at[1 - side],
            device_id={"brick": peer_of[side]},
            device_id_type=MESH,
        )

    def partial_in(side):
        return pltpu.make_async_remote_copy(
            src_ref=part.at[2 + side],
            dst_ref=part.at[2 + side],
            send_sem=part_send.at[side],
            recv_sem=part_recv.at[side],
            device_id={"brick": peer_of[side]},
            device_id_type=MESH,
        )

    for side in range(2):
        part[side] = to_coarse(ry[...], rz, X[2 * side])

    for side in range(2):

        @pl.when(has[side])
        def _():
            partial(side).start()

        @pl.when(jnp.logical_not(has[side]))
        def _():
            part[2 + side] = jnp.zeros(part.shape[1:], F32)

    mine = to_coarse(ry[...], rz, X[1])
    for side in range(2):

        @pl.when(has[side])
        def _():
            partial_in(side).wait_recv()

    all_r[me] = (mine + (part[2] + part[3])) * (1.0 / 64.0)
    spread(all_r, r_send, r_recv)

    hand_on(all_q, q_send, q_recv)
    collect(all_q, q_send, q_recv)
    coarse_coefficients(n, min(8, n), all_q, q_pad, coef, scaled)
    hand_on(all_r, r_send, r_recv)

    rows, lanes = all_r.shape[1:]
    shifts, _ = coarse_shifts((group, rows, lanes))
    edge = jnp.zeros((rows, lanes), F32)
    for slot in range(2):
        C[slot, 0] = edge
        C[slot, n + 1] = edge
    collect(all_r, r_send, r_recv)
    B[...] = all_r[...] * scaled[...]
    C[0, 1 : n + 1] = B[...]

    for sweep in range(SWEEPS - 1):
        now, later = sweep % 2, 1 - sweep % 2

        def step(g, _):
            at = pl.multiple_of(g * group, group)
            c = C[now, pl.ds(at + 1, group)]
            near = (C[now, pl.ds(at, group)], C[now, pl.ds(at + 2, group)]) + shifts(c)
            terms = [coef[k, pl.ds(at, group)] * v for k, v in enumerate(near)]
            total = B[pl.ds(at, group)] + 0.2 * c
            total = (total + (terms[0] + terms[1])) + ((terms[2] + terms[3]) + (terms[4] + terms[5]))
            C[later, pl.ds(at + 1, group)] = total
            return 0

        lax.fori_loop(0, n // group, step, 0)

    for side in range(2):

        @pl.when(has[side])
        def _():
            for c in range(CHUNKS):
                for which in range(3):
                    halo(which, side, c).wait_send()
            partial(side).wait_send()

    sent(all_q, q_send, q_recv)
    sent(all_r, r_send, r_recv)


def coarse_shifts(shape):
    rows, lanes = shape[1:]
    cz = lanes // 2
    row = lax.broadcasted_iota(jnp.int32, shape, 1)
    lane = lax.broadcasted_iota(jnp.int32, shape, 2)
    low_half = lane < cz
    z = jnp.where(low_half, lane, lane - cz)
    outside = (
        (row == 0) & low_half,
        (row == rows - 1) & jnp.logical_not(low_half),
        z == 0,
        z == cz - 1,
    )

    def shifts(c):
        swapped = pltpu.roll(c, cz, 2)
        y_low = jnp.where(low_half, pltpu.roll(swapped, 1, 1), swapped)
        y_high = jnp.where(low_half, swapped, pltpu.roll(swapped, rows - 1, 1))
        return y_low, y_high, pltpu.roll(c, 1, 2), pltpu.roll(c, lanes - 1, 2)

    return shifts, outside


def coarse_coefficients(n, group, perm, q_pad, coef, scaled):
    rows, lanes = perm.shape[1:]
    shifts, outside = coarse_shifts((group, rows, lanes))
    edge = jnp.zeros((rows, lanes), F32)
    q_pad[0] = edge
    q_pad[n + 1] = edge
    q_pad[1 : n + 1] = perm[...]

    def prepare(g, _):
        at = pl.multiple_of(g * group, group)
        q = q_pad[pl.ds(at + 1, group)]
        near = [q_pad[pl.ds(at, group)], q_pad[pl.ds(at + 2, group)]]
        near += [jnp.where(out, 0.0, v) for out, v in zip(outside, shifts(q))]
        faces = [0.5 * (q + v) for v in near]
        diagonal = ((faces[0] + faces[1]) + (faces[2] + faces[3])) + (faces[4] + faces[5])
        scale = 0.8 / diagonal
        for k, out in enumerate((None, None) + outside):
            f = faces[k] * scale
            coef[k, pl.ds(at, group)] = f if out is None else jnp.where(out, 0.0, f)
        scaled[pl.ds(at, group)] = 16.0 * scale
        return 0

    lax.fori_loop(0, n // group, prepare, 0)


def prolong_kernel(n, C, U2, ez, ey, holder, corrected_hbm, held_hbm, corrected, held, sem):
    me = lax.axis_index("brick")
    rows, lanes = C.shape[2:]
    ny = corrected.shape[1]
    final = (SWEEPS - 1) % 2
    below, mid, above = C[final, me], C[final, me + 1], C[final, me + 2]
    planes = jnp.concatenate(
        [
            0.625 * mid + 0.375 * below,
            0.875 * mid + 0.125 * below,
            0.875 * mid + 0.125 * above,
            0.625 * mid + 0.375 * above,
        ],
        axis=0,
    )
    hi, lo = split(planes)
    even = dot(hi, ez[0]) + dot(lo, ez[0])
    odd = dot(hi, ez[1]) + dot(lo, ez[1])
    copies = []
    for p in range(4):
        both = jnp.concatenate(
            [even[p * rows : (p + 1) * rows], odd[p * rows : (p + 1) * rows]], axis=0
        )
        hi, lo = split(both)
        corrected[p] = U2[p, 8 : ny + 8] + (dot(ey[...], hi) + dot(ey[...], lo))
        copies.append(pltpu.make_async_copy(corrected.at[p], corrected_hbm.at[p], sem.at[p]))
        copies[p].start()

    mine = jnp.zeros((rows, lanes), F32)
    for b in range(n):
        mine = jnp.where(holder[b : b + 1] == me, C[final, b + 1], mine)
    for r in range(rows):
        held[0:1, r * lanes : (r + 1) * lanes] = mine[r : r + 1]
    copies.append(pltpu.make_async_copy(held, held_hbm, sem.at[4]))
    copies[4].start()
    for copy in copies:
        copy.wait()


def local(n, source, guess, log_perm, owner):
    planes, ny, nz = source.shape
    assert planes == 4 and n % 2 == 0
    cells = (ny // 4) * (nz // 4)
    rows, lanes = ny // 8, nz // 2
    assert lanes == 128
    dense = (rows, lanes)
    as_bf16 = lambda m: jnp.asarray(m.astype(ml_dtypes.bfloat16))
    py, pz = even_odd(prolong_matrix(ny)), prolong_matrix(nz)
    ry, rz = as_bf16(py.T), as_bf16(halves(pz))
    my, mz = as_bf16(even_odd(mean_matrix(ny)).T), as_bf16(halves(mean_matrix(nz)))
    ey, ez = as_bf16(py), as_bf16(halves(pz).transpose(0, 2, 1))
    vmem = pl.BlockSpec(memory_space=pltpu.VMEM)
    hbm = pl.BlockSpec(memory_space=pl.ANY)
    whole = lambda *s: pltpu.VMEM(s, F32)
    dma = lambda *s: pltpu.SemaphoreType.DMA(s)
    padded = (4, ny + 16, nz)
    kept = pl.pallas_call(
        functools.partial(smooth_kernel, n, ny, nz, min(16, n)),
        out_shape=(
            whole(*padded), whole(2, n + 2, *dense), pltpu.VMEM(ez.shape, BF16), pltpu.VMEM(ey.shape, BF16),
            pltpu.VMEM((n, 128), jnp.int32),
        ),
        in_specs=[hbm] * 10,
        out_specs=(vmem,) * 5,
        scratch_shapes=[
            pltpu.SMEM((n,), jnp.int32),
            whole(6, n, *dense), whole(n, *dense),
            pltpu.VMEM(ry.shape, BF16), pltpu.VMEM(rz.shape, BF16),
            pltpu.VMEM(my.shape, BF16), pltpu.VMEM(mz.shape, BF16),
            whole(n, *dense), whole(n + 2, *dense), whole(n, *dense), whole(n, *dense),
            whole(4, ny, nz), whole(4, ny, nz),
            whole(*padded), whole(*padded), whole(*padded),
            whole(4, ny, nz), whole(4, ny, nz), whole(4, ny, nz),
            whole(2, ny, nz), whole(3, ny, nz), whole(3, 2, ny, nz),
            whole(4, *dense),
            dma(10), dma(3, 2, CHUNKS), dma(3, 2, CHUNKS), dma(2), dma(2),
            dma(n), dma(n), dma(n), dma(n),
            pltpu.SemaphoreType.REGULAR(((n - 1).bit_length(),)),
        ],
        compiler_params=pltpu.CompilerParams(
            collective_id=0, has_side_effects=True, vmem_limit_bytes=28 * 2**20
        ),
        name="smooth",
    )(*(pltpu.with_memory_space_constraint(a, pltpu.HBM) for a in (source, guess, log_perm, owner, ry, rz, my, mz, ez, ey)))
    smooth, coarse, ez, ey, holder = [pltpu.with_memory_space_constraint(a, pltpu.VMEM) for a in kept]
    return pl.pallas_call(
        functools.partial(prolong_kernel, n),
        out_shape=(
            jax.ShapeDtypeStruct((4, ny, nz), F32),
            jax.ShapeDtypeStruct((1, cells), F32),
        ),
        in_specs=[vmem] * 5,
        out_specs=(hbm, hbm),
        scratch_shapes=[whole(4, ny, nz), whole(1, cells), dma(5)],
        compiler_params=pltpu.CompilerParams(vmem_limit_bytes=16 * 2**20),
        name="prolong",
    )(coarse, smooth, ez, ey, holder)


def solution(mesh):
    spec = P(("samples", "brick"), None, None)
    return jax.shard_map(
        functools.partial(local, mesh.shape["brick"]),
        mesh=mesh,
        in_specs=(spec, spec, spec, P()),
        out_specs=(spec, P(("samples", "brick"), None)),
        check_vma=False,
    )
```

time: 30.5 us -> 28.3 us (0.928); the launches traced: 30 us -> 28.1 us
  Pallas kernels: 29.3 us -> 27.5 us
    pallas_call x2, Pallas kernels: 29.3 us -> 27.5 us  [the longest x1 26.3 us: local(): pl.pallas_call(functools.partial(smooth_kernel, n, ny, nz, min(16, n)), o...]
where the time goes in v1:
time: 28.3 us; the launch traced here: 28.1 us
  Pallas kernels  27.5 us (97%)
  between operations  0.64 us (2%)
    pallas_call x1, Pallas kernels, local(): pl.pallas_call(functools.partial(smooth_kernel, n, ny, nz, min(16, n)), o...  26.3 us
    pallas_call x1, Pallas kernels, local(): pl.pallas_call(functools.partial(prolong_kernel, n), out_shape=(jax.Shape...  1.19 us

profile of v1, /device:TPU:1, one launch (start us, length us, event | category | flops | bytes accessed | tf_op | source)
XLA Modules:
  0.0 28.1 jit_solution(14442001360757137298)
XLA Ops:
  0.6 26.3 %smooth.1 = (f32[4,144,256]{2,1,0:T(8,128)S(1)}, f32[2,18,16,128]{3,2,1,0:T(8,128)S(1)}, bf16[2,128,256]{2,1,0:T(8,128)(2,1)S(1)}, bf16[128,32]{1,0:T(8,128)(2,1)S(1)}, s32[16,128]{1,0:T(8,128)S(1)}) custom-call(f32[4,128,256]{2,1,0:T(8,128)} %source_hbm.1, f32[4,128,256]{2,1,0:T(8,128)} %guess_hbm.1, f32[4,128,256]{2,1,0:T(8,128)} %logq_hbm.1, ...), custom_call_target="tpu_custom_call" | custom-call | tf_op jit(solution)/shard_map/smooth/pallas_call | solution.py:575
  26.9 1.2 %prolong.1 = (f32[4,128,256]{2,1,0:T(8,128)}, f32[1,2048]{1,0:T(1,128)}) custom-call(f32[2,18,16,128]{3,2,1,0:T(8,128)S(1)} %get-tuple-element.7.C, f32[4,144,256]{2,1,0:T(8,128)S(1)} %get-tuple-element.8.U2, bf16[2,128,256]{2,1,0:T(8,128)(2,1)S(1)} %get-tuple-element.9.ez, bf16[128,32]{1,0:T(8,128)(2,1)S(1)} %get-tuple-element.10.ey, ...), custom_call_target="tpu_custom_call" | custom-call | tf_op jit(solution)/shard_map/prolong/pallas_call | solution.py:604

commit v2 on v1

--- a/solution.py
+++ b/solution.py
@@ -11,6 +11,7 @@
 
 SWEEPS = 8
 CHUNKS = 8
+FIRST = 4
 MESH = pl.DeviceIdType.MESH
 F32 = jnp.float32
 BF16 = jnp.bfloat16
@@ -61,30 +62,32 @@
 
 def smooth_kernel(
     n, ny, nz, group,
-    source_hbm, guess_hbm, logq_hbm, owner_hbm, ry_hbm, rz_hbm, my_hbm, mz_hbm, ez_hbm, ey_hbm,
+    source_hbm, guess_hbm, logq_hbm, owner_hbm, y_hbm, z_hbm, ez_hbm, ey_hbm,
     U2, C, ez, ey, holder,
-    owner, coef, scaled, ry, rz, my, mz, all_q, q_pad, all_r, B, src, logq, K, U0, U1, D, W, N, F, X, H, part,
-    local_sem, halo_send, halo_recv, part_send, part_recv, q_send, q_recv, r_send, r_recv, token_sem,
+    owner, coef, scaled, ymat, zmat, all_q, q_pad, all_r, B, src, logq, K, U0, U1, D, W, N, F, X, H, part,
+    local_sem, halo_send, first_recv, second_recv, part_send, part_recv, q_send, q_recv, r_send, r_recv, token_sem,
 ):
     me = lax.axis_index("brick")
     R = ny // CHUNKS
     half = n // 2
     has = (me > 0, me < n - 1)
     flag = [jnp.where(h, 1.0, 0.0).astype(F32) for h in has]
-    peer_of = (me - 1, me + 1)
-    sibling = me + 1 - 2 * lax.rem(me, 2)
+    far = lax.rem(me, 2)
+    near_side = 1 - far
+    sibling = me + 1 - 2 * far
+    mine_at = (far, me // 2)
+    neighbour = lambda side: me - 1 + 2 * side
+    exists = lambda side: jnp.logical_and(neighbour(side) >= 0, neighbour(side) < n)
 
     loads = [
         pltpu.make_async_copy(logq_hbm, logq, local_sem.at[0]),
         pltpu.make_async_copy(guess_hbm, U0.at[:, pl.ds(8, ny)], local_sem.at[1]),
         pltpu.make_async_copy(source_hbm, src, local_sem.at[2]),
-        pltpu.make_async_copy(my_hbm, my, local_sem.at[3]),
-        pltpu.make_async_copy(mz_hbm, mz, local_sem.at[4]),
-        pltpu.make_async_copy(ry_hbm, ry, local_sem.at[5]),
-        pltpu.make_async_copy(rz_hbm, rz, local_sem.at[6]),
-        pltpu.make_async_copy(ez_hbm, ez, local_sem.at[7]),
-        pltpu.make_async_copy(ey_hbm, ey, local_sem.at[8]),
-        pltpu.make_async_copy(owner_hbm, owner, local_sem.at[9]),
+        pltpu.make_async_copy(y_hbm, ymat, local_sem.at[3]),
+        pltpu.make_async_copy(z_hbm, zmat, local_sem.at[4]),
+        pltpu.make_async_copy(ez_hbm, ez, local_sem.at[5]),
+        pltpu.make_async_copy(ey_hbm, ey, local_sem.at[6]),
+        pltpu.make_async_copy(owner_hbm, owner, local_sem.at[7]),
     ]
 
     def signal(sem, who):
@@ -107,6 +110,12 @@
         pl.semaphore_wait(sem, low + high)
 
     distances = [2**k for k in range((n - 1).bit_length())]
+
+    def relay(k):
+        if k < len(distances):
+            greeted(token_sem.at[k], distances[k])
+        if k + 1 < len(distances):
+            greet(token_sem.at[k + 1], distances[k + 1])
 
     greet(barrier, 1)
     for copy in loads:
@@ -125,6 +134,7 @@
                 H[which, side] = jnp.zeros((ny, nz), F32)
 
     greeted(barrier, 1)
+    greet(token_sem.at[0], 1)
 
     def rows_at(c):
         return pl.ds(c * R if isinstance(c, int) else pl.multiple_of(c * R, R), R)
@@ -132,41 +142,71 @@
     def rows_in(c):
         return pl.ds(8 + c * R if isinstance(c, int) else pl.multiple_of(c * R, R) + 8, R)
 
-    def halo(which, side, c):
-        plane = 3 * side
-        if which == 2:
-            ref = U1.at[plane, rows_in(c)]
-        else:
-            ref = (logq_hbm, guess_hbm)[which].at[plane, rows_at(c)]
-        return pltpu.make_async_remote_copy(
-            src_ref=ref,
-            dst_ref=H.at[which, 1 - side, rows_at(c)],
-            send_sem=halo_send.at[which, side, c],
-            recv_sem=halo_recv.at[which, 1 - side, c],
-            device_id={"brick": peer_of[side]},
-            device_id_type=MESH,
-        )
-
-    def arrival(which, side, c):
-        ref = H.at[which, side, rows_at(c)]
+    Q = ny // FIRST
+
+    def send_first(side):
+        for c in range(FIRST):
+            rows = pl.ds(c * Q, Q)
+            for which, ref in enumerate((logq_hbm, guess_hbm)):
+                pltpu.make_async_remote_copy(
+                    src_ref=ref.at[3 * side, rows],
+                    dst_ref=H.at[which, 1 - side, rows],
+                    send_sem=halo_send.at[side],
+                    recv_sem=first_recv.at[1 - side, c],
+                    device_id={"brick": neighbour(side)},
+                    device_id_type=MESH,
+                ).start()
+
+    def first_in(side, c):
+        ref = H.at[0:2, side, pl.ds(pl.multiple_of(c * Q, Q), Q)]
         return pltpu.make_async_remote_copy(
             src_ref=ref,
             dst_ref=ref,
-            send_sem=halo_send.at[which, side, c],
-            recv_sem=halo_recv.at[which, side, c],
-            device_id={"brick": peer_of[side]},
-            device_id_type=MESH,
-        )
-
-    for c in range(CHUNKS):
-        for side in range(2):
-
-            @pl.when(has[side])
-            def _():
-                halo(0, side, c).start()
-                halo(1, side, c).start()
-
-    greet(token_sem.at[0], 1)
+            send_sem=halo_send.at[side],
+            recv_sem=first_recv.at[side, c],
+            device_id={"brick": neighbour(side)},
+            device_id_type=MESH,
+        )
+
+    def second(side, c):
+        return pltpu.make_async_remote_copy(
+            src_ref=U1.at[3 * side, rows_in(c)],
+            dst_ref=H.at[2, 1 - side, rows_at(c)],
+            send_sem=halo_send.at[side],
+            recv_sem=second_recv.at[1 - side, c],
+            device_id={"brick": neighbour(side)},
+            device_id_type=MESH,
+        )
+
+    def second_in(side, c):
+        ref = H.at[2, side, rows_at(c)]
+        return pltpu.make_async_remote_copy(
+            src_ref=ref,
+            dst_ref=ref,
+            send_sem=halo_send.at[side],
+            recv_sem=second_recv.at[side, c],
+            device_id={"brick": neighbour(side)},
+            device_id_type=MESH,
+        )
+
+    def halo_sent(side):
+        ref = H.at[:, side]
+        return pltpu.make_async_remote_copy(
+            src_ref=ref,
+            dst_ref=ref,
+            send_sem=halo_send.at[side],
+            recv_sem=first_recv.at[side, 0],
+            device_id={"brick": neighbour(side)},
+            device_id_type=MESH,
+        )
+
+    for side in (far, near_side):
+
+        @pl.when(exists(side))
+        def _():
+            send_first(side)
+
+    relay(0)
 
     lane = lax.broadcasted_iota(jnp.int32, (R, nz), 1)
     first, last = lane == 0, lane == nz - 1
@@ -198,6 +238,7 @@
     lax.fori_loop(0, CHUNKS, exps, 0)
     for copy in loads[1:]:
         copy.wait()
+    relay(1)
 
     def windows(ref, c):
         at = pl.ds(pl.multiple_of(c * R, R), R + 16)
@@ -224,18 +265,14 @@
         return 0
 
     lax.fori_loop(0, CHUNKS, sweep_one, 0)
-    greeted(token_sem.at[0], 1)
-
-    all_q[me] = to_coarse(
-        my[...], mz, (K[0, 8 : ny + 8] + K[1, 8 : ny + 8]) + (K[2, 8 : ny + 8] + K[3, 8 : ny + 8])
+
+    all_q[mine_at] = to_coarse(
+        ymat[0], zmat[0:2], (K[0, 8 : ny + 8] + K[1, 8 : ny + 8]) + (K[2, 8 : ny + 8] + K[3, 8 : ny + 8])
     ) * (1.0 / 64.0)
     for b in range(n):
         holder[b : b + 1] = jnp.full((1, 128), owner[b], jnp.int32)
 
-    for k in range(1, len(distances)):
-        greet(token_sem.at[k], distances[k])
-        if k + 1 < len(distances):
-            greeted(token_sem.at[k], distances[k])
+    relay(2)
 
     def finish_one(c):
         rows, at = rows_at(c), rows_in(c)
@@ -243,8 +280,10 @@
 
             @pl.when(has[side])
             def _():
-                arrival(0, side, c).wait_recv()
-                arrival(1, side, c).wait_recv()
+
+                @pl.when(lax.rem(c, CHUNKS // FIRST) == 0)
+                def _():
+                    first_in(side, c // (CHUNKS // FIRST)).wait_recv()
 
         for side in range(2):
             p = 3 * side
@@ -256,65 +295,75 @@
             D[p, rows] = d
             W[p, rows] = w
             U1[p, at] = 0.2 * U0[p, at] + w * (N[p, rows] + face * H[1, side, rows])
-        for side in range(2):
-
-            @pl.when(has[side])
+        for side in (far, near_side):
+
+            @pl.when(exists(side))
             def _():
-                halo(2, side, c).start()
-
-    def copy_to(ref, slot, who, send, recv):
-        return pltpu.make_async_remote_copy(
-            src_ref=ref.at[slot],
-            dst_ref=ref.at[slot],
-            send_sem=send,
-            recv_sem=recv.at[slot],
-            device_id={"brick": who},
-            device_id_type=MESH,
-        )
+                second(side, c).start()
 
     def direct(ref, j, send, recv):
-        return copy_to(ref, me, lax.rem(me + 2 * j, n), send.at[j], recv)
-
-    def handed(ref, j, send, recv):
-        who = lax.rem(me + n - 2 * j, n)
-        return copy_to(ref, who, sibling, send.at[half + j], recv)
-
-    def to_sibling(ref, send, recv):
-        return copy_to(ref, me, sibling, send.at[0], recv)
-
-    def spread(ref, send, recv):
-        def body(j, _):
-            direct(ref, j, send, recv).start()
+        return pltpu.make_async_remote_copy(
+            src_ref=ref.at[mine_at],
+            dst_ref=ref.at[mine_at],
+            send_sem=send.at[1],
+            recv_sem=recv,
+            device_id={"brick": lax.rem(me + 2 * j, n)},
+            device_id_type=MESH,
+        )
+
+    def to_sibling(ref, part_of, send, recv):
+        return pltpu.make_async_remote_copy(
+            src_ref=ref.at[part_of],
+            dst_ref=ref.at[part_of],
+            send_sem=send.at[0],
+            recv_sem=recv,
+            device_id={"brick": sibling},
+            device_id_type=MESH,
+        )
+
+    def repeat(low, body):
+        def step(j, _):
+            body(j)
             return 0
 
-        lax.fori_loop(1, half, body, 0)
-        to_sibling(ref, send, recv).start()
-
-    def hand_on(ref, send, recv):
-        def body(j, _):
-            copy = handed(ref, j, send, recv)
-            copy.wait_recv()
-            copy.start()
-            return 0
-
-        lax.fori_loop(1, half, body, 0)
-
-    def collect(ref, send, recv):
-        def body(j, _):
-            slot = lax.rem(sibling + n - 2 * j, n)
-            copy_to(ref, slot, sibling, send.at[half + j], recv).wait_recv()
-            return 0
-
-        lax.fori_loop(0, half, body, 0)
+        lax.fori_loop(low, half, step, 0)
+
+    def from_sibling(ref, send, recv):
+        to_sibling(ref, 1 - far, send, recv).wait_recv()
 
     def sent(ref, send, recv):
-        def body(j, _):
-            direct(ref, j, send, recv).wait_send()
-            handed(ref, j, send, recv).wait_send()
-            return 0
-
-        lax.fori_loop(1, half, body, 0)
-        to_sibling(ref, send, recv).wait_send()
+        for side, blocks in ((0, half), (1, half - 1)):
+            part_of = ref.at[side, 0:blocks]
+            pltpu.make_async_remote_copy(
+                src_ref=part_of, dst_ref=part_of, send_sem=send.at[side], recv_sem=recv,
+                device_id={"brick": sibling}, device_id_type=MESH,
+            ).wait_send()
+
+    def spread_q():
+        repeat(1, lambda j: direct(all_q, j, q_send, q_recv.at[0]).start())
+
+    def hand_on_q():
+        ref = all_q.at[0, 0 : half - 1]
+        pltpu.make_async_remote_copy(
+            src_ref=ref, dst_ref=ref, send_sem=q_send.at[0], recv_sem=q_recv.at[0],
+            device_id={"brick": sibling}, device_id_type=MESH,
+        ).wait_recv()
+        to_sibling(all_q, far, q_send, q_recv.at[1]).start()
+
+    def r_place(j):
+        return far, lax.rem(me // 2 + half - j, half)
+
+    def spread_r():
+        repeat(1, lambda j: direct(all_r, j, r_send, r_recv.at[me // 2]).start())
+        to_sibling(all_r, mine_at, r_send, r_recv.at[half]).start()
+
+    def hand_on_r():
+        def step(j):
+            place = r_place(j)
+            to_sibling(all_r, place, r_send, r_recv.at[place[1]]).wait_recv()
+            to_sibling(all_r, place, r_send, r_recv.at[half]).start()
+
+        repeat(1, step)
 
     def sweep_two(c):
         rows, at = rows_at(c), rows_in(c)
@@ -327,15 +376,22 @@
             else:
                 U2[p, at] = 0.2 * middle(u[p]) + W[p, rows] * total
 
+    relays = range(3, len(distances))
+
     def first_stage(c, _):
         @pl.when(c < CHUNKS)
         def _():
             finish_one(c)
 
+        for k in relays:
+
+            @pl.when(c == CHUNKS - 1 - (relays[-1] - k))
+            def _():
+                relay(k)
+
         @pl.when(c == CHUNKS - 1)
         def _():
-            greeted(token_sem.at[len(distances) - 1], distances[-1])
-            spread(all_q, q_send, q_recv)
+            spread_q()
 
         @pl.when(c > 0)
         def _():
@@ -351,7 +407,7 @@
 
             @pl.when(has[side])
             def _():
-                arrival(2, side, c).wait_recv()
+                second_in(side, c).wait_recv()
 
         for side in range(2):
             p = 3 * side
@@ -388,7 +444,7 @@
             dst_ref=part.at[3 - side],
             send_sem=part_send.at[side],
             recv_sem=part_recv.at[1 - side],
-            device_id={"brick": peer_of[side]},
+            device_id={"brick": neighbour(side)},
             device_id_type=MESH,
         )
 
@@ -398,12 +454,12 @@
             dst_ref=part.at[2 + side],
             send_sem=part_send.at[side],
             recv_sem=part_recv.at[side],
-            device_id={"brick": peer_of[side]},
+            device_id={"brick": neighbour(side)},
             device_id_type=MESH,
         )
 
     for side in range(2):
-        part[side] = to_coarse(ry[...], rz, X[2 * side])
+        part[side] = to_coarse(ymat[1], zmat[2:4], X[2 * side])
 
     for side in range(2):
 
@@ -415,30 +471,32 @@
         def _():
             part[2 + side] = jnp.zeros(part.shape[1:], F32)
 
-    mine = to_coarse(ry[...], rz, X[1])
+    mine = to_coarse(ymat[1], zmat[2:4], X[1])
+    hand_on_q()
     for side in range(2):
 
         @pl.when(has[side])
         def _():
             partial_in(side).wait_recv()
 
-    all_r[me] = (mine + (part[2] + part[3])) * (1.0 / 64.0)
-    spread(all_r, r_send, r_recv)
-
-    hand_on(all_q, q_send, q_recv)
-    collect(all_q, q_send, q_recv)
+    all_r[mine_at] = (mine + (part[2] + part[3])) * (1.0 / 64.0)
+    spread_r()
+
+    from_sibling(all_q, q_send, q_recv.at[1])
     coarse_coefficients(n, min(8, n), all_q, q_pad, coef, scaled)
-    hand_on(all_r, r_send, r_recv)
-
-    rows, lanes = all_r.shape[1:]
+    hand_on_r()
+
+    rows, lanes = all_r.shape[2:]
     shifts, _ = coarse_shifts((group, rows, lanes))
     edge = jnp.zeros((rows, lanes), F32)
     for slot in range(2):
         C[slot, 0] = edge
         C[slot, n + 1] = edge
-    collect(all_r, r_send, r_recv)
-    B[...] = all_r[...] * scaled[...]
-    C[0, 1 : n + 1] = B[...]
+    from_sibling(all_r, r_send, r_recv.at[half])
+    for b in range(n):
+        scaled_rhs = all_r[b % 2, b // 2] * scaled[b]
+        B[b] = scaled_rhs
+        C[0, b + 1] = scaled_rhs
 
     for sweep in range(SWEEPS - 1):
         now, later = sweep % 2, 1 - sweep % 2
@@ -459,13 +517,11 @@
 
         @pl.when(has[side])
         def _():
-            for c in range(CHUNKS):
-                for which in range(3):
-                    halo(which, side, c).wait_send()
+            halo_sent(side).wait_send()
             partial(side).wait_send()
 
-    sent(all_q, q_send, q_recv)
-    sent(all_r, r_send, r_recv)
+    sent(all_q, q_send, q_recv.at[0])
+    sent(all_r, r_send, r_recv.at[0])
 
 
 def coarse_shifts(shape):
@@ -492,12 +548,13 @@
 
 
 def coarse_coefficients(n, group, perm, q_pad, coef, scaled):
-    rows, lanes = perm.shape[1:]
+    rows, lanes = perm.shape[2:]
     shifts, outside = coarse_shifts((group, rows, lanes))
     edge = jnp.zeros((rows, lanes), F32)
     q_pad[0] = edge
     q_pad[n + 1] = edge
-    q_pad[1 : n + 1] = perm[...]
+    for b in range(n):
+        q_pad[b + 1] = perm[b % 2, b // 2]
 
     def prepare(g, _):
         at = pl.multiple_of(g * group, group)
@@ -564,8 +621,8 @@
     dense = (rows, lanes)
     as_bf16 = lambda m: jnp.asarray(m.astype(ml_dtypes.bfloat16))
     py, pz = even_odd(prolong_matrix(ny)), prolong_matrix(nz)
-    ry, rz = as_bf16(py.T), as_bf16(halves(pz))
-    my, mz = as_bf16(even_odd(mean_matrix(ny)).T), as_bf16(halves(mean_matrix(nz)))
+    ymat = as_bf16(np.stack([even_odd(mean_matrix(ny)).T, py.T]))
+    zmat = as_bf16(np.concatenate([halves(mean_matrix(nz)), halves(pz)]))
     ey, ez = as_bf16(py), as_bf16(halves(pz).transpose(0, 2, 1))
     vmem = pl.BlockSpec(memory_space=pltpu.VMEM)
     hbm = pl.BlockSpec(memory_space=pl.ANY)
@@ -578,28 +635,27 @@
             whole(*padded), whole(2, n + 2, *dense), pltpu.VMEM(ez.shape, BF16), pltpu.VMEM(ey.shape, BF16),
             pltpu.VMEM((n, 128), jnp.int32),
         ),
-        in_specs=[hbm] * 10,
+        in_specs=[hbm] * 8,
         out_specs=(vmem,) * 5,
         scratch_shapes=[
             pltpu.SMEM((n,), jnp.int32),
             whole(6, n, *dense), whole(n, *dense),
-            pltpu.VMEM(ry.shape, BF16), pltpu.VMEM(rz.shape, BF16),
-            pltpu.VMEM(my.shape, BF16), pltpu.VMEM(mz.shape, BF16),
-            whole(n, *dense), whole(n + 2, *dense), whole(n, *dense), whole(n, *dense),
+            pltpu.VMEM(ymat.shape, BF16), pltpu.VMEM(zmat.shape, BF16),
+            whole(2, n // 2, *dense), whole(n + 2, *dense), whole(2, n // 2, *dense), whole(n, *dense),
             whole(4, ny, nz), whole(4, ny, nz),
             whole(*padded), whole(*padded), whole(*padded),
             whole(4, ny, nz), whole(4, ny, nz), whole(4, ny, nz),
             whole(2, ny, nz), whole(3, ny, nz), whole(3, 2, ny, nz),
             whole(4, *dense),
-            dma(10), dma(3, 2, CHUNKS), dma(3, 2, CHUNKS), dma(2), dma(2),
-            dma(n), dma(n), dma(n), dma(n),
+            dma(8), dma(2), dma(2, FIRST), dma(2, CHUNKS), dma(2), dma(2),
+            dma(2), dma(2), dma(2), dma(n // 2 + 1),
             pltpu.SemaphoreType.REGULAR(((n - 1).bit_length(),)),
         ],
         compiler_params=pltpu.CompilerParams(
             collective_id=0, has_side_effects=True, vmem_limit_bytes=28 * 2**20
         ),
         name="smooth",
-    )(*(pltpu.with_memory_space_constraint(a, pltpu.HBM) for a in (source, guess, log_perm, owner, ry, rz, my, mz, ez, ey)))
+    )(*(pltpu.with_memory_space_constraint(a, pltpu.HBM) for a in (source, guess, log_perm, owner, ymat, zmat, ez, ey)))
     smooth, coarse, ez, ey, holder = [pltpu.with_memory_space_constraint(a, pltpu.VMEM) for a in kept]
     return pl.pallas_call(
         functools.partial(prolong_kernel, n),

time: 28.3 us -> 27.2 us (0.961)
  Pallas kernels: 27.5 us -> 26.4 us
    pallas_call x1, Pallas kernels: 26.3 us -> 25.2 us  [local(): pl.pallas_call(functools.partial(smooth_kernel, n, ny, nz, min(16, n)), o...]
where the time goes in v2:
time: 27.2 us; the launch traced here: 27 us
  Pallas kernels  26.4 us (97%)
  between operations  0.64 us (2%)
    pallas_call x1, Pallas kernels, local(): pl.pallas_call(functools.partial(smooth_kernel, n, ny, nz, min(16, n)), o...  25.2 us
    pallas_call x1, Pallas kernels, local(): pl.pallas_call(functools.partial(prolong_kernel, n), out_shape=(jax.Shape...  1.19 us

profile of v2, /device:TPU:1, one launch (start us, length us, event | category | flops | bytes accessed | tf_op | source)
XLA Modules:
  0.0 27.0 jit_solution(483449305121409464)
XLA Ops:
  0.6 25.2 %smooth.1 = (f32[4,144,256]{2,1,0:T(8,128)S(1)}, f32[2,18,16,128]{3,2,1,0:T(8,128)S(1)}, bf16[2,128,256]{2,1,0:T(8,128)(2,1)S(1)}, bf16[128,32]{1,0:T(8,128)(2,1)S(1)}, s32[16,128]{1,0:T(8,128)S(1)}) custom-call(f32[4,128,256]{2,1,0:T(8,128)} %source_hbm.1, f32[4,128,256]{2,1,0:T(8,128)} %guess_hbm.1, f32[4,128,256]{2,1,0:T(8,128)} %logq_hbm.1, ...), custom_call_target="tpu_custom_call" | custom-call | tf_op jit(solution)/shard_map/smooth/pallas_call | solution.py:632
  25.8 1.2 %prolong.1 = (f32[4,128,256]{2,1,0:T(8,128)}, f32[1,2048]{1,0:T(1,128)}) custom-call(f32[2,18,16,128]{3,2,1,0:T(8,128)S(1)} %get-tuple-element.7.C, f32[4,144,256]{2,1,0:T(8,128)S(1)} %get-tuple-element.8.U2, bf16[2,128,256]{2,1,0:T(8,128)(2,1)S(1)} %get-tuple-element.9.ez, bf16[128,32]{1,0:T(8,128)(2,1)S(1)} %get-tuple-element.10.ey, ...), custom_call_target="tpu_custom_call" | custom-call | tf_op jit(solution)/shard_map/prolong/pallas_call | solution.py:660

commit v3 on v2

--- a/solution.py
+++ b/solution.py
@@ -64,8 +64,8 @@
     n, ny, nz, group,
     source_hbm, guess_hbm, logq_hbm, owner_hbm, y_hbm, z_hbm, ez_hbm, ey_hbm,
     U2, C, ez, ey, holder,
-    owner, coef, scaled, ymat, zmat, all_q, q_pad, all_r, B, src, logq, K, U0, U1, D, W, N, F, X, H, part,
-    local_sem, halo_send, first_recv, second_recv, part_send, part_recv, q_send, q_recv, r_send, r_recv, token_sem,
+    owner, coef, scaled, ymat, zmat, all_q, q_pad, all_p, all_r, B, src, logq, K, U0, U1, D, W, N, F, X, H, part,
+    local_sem, halo_send, first_recv, second_recv, part_sem, q_send, q_recv, p_send, p_recv, r_send, r_recv, token_sem,
 ):
     me = lax.axis_index("brick")
     R = ny // CHUNKS
@@ -301,16 +301,6 @@
             def _():
                 second(side, c).start()
 
-    def direct(ref, j, send, recv):
-        return pltpu.make_async_remote_copy(
-            src_ref=ref.at[mine_at],
-            dst_ref=ref.at[mine_at],
-            send_sem=send.at[1],
-            recv_sem=recv,
-            device_id={"brick": lax.rem(me + 2 * j, n)},
-            device_id_type=MESH,
-        )
-
     def to_sibling(ref, part_of, send, recv):
         return pltpu.make_async_remote_copy(
             src_ref=ref.at[part_of],
@@ -321,49 +311,47 @@
             device_id_type=MESH,
         )
 
-    def repeat(low, body):
+    def others(body):
         def step(j, _):
-            body(j)
+            body(j + jnp.where(j >= me // 2, 1, 0))
             return 0
 
-        lax.fori_loop(low, half, step, 0)
+        lax.fori_loop(0, half - 1, step, 0)
+
+    def spread(ref, send, recv):
+        def step(k):
+            pltpu.make_async_remote_copy(
+                src_ref=ref.at[mine_at],
+                dst_ref=ref.at[mine_at],
+                send_sem=send.at[1],
+                recv_sem=recv,
+                device_id={"brick": 2 * k + far},
+                device_id_type=MESH,
+            ).start()
+
+        others(step)
 
     def from_sibling(ref, send, recv):
         to_sibling(ref, 1 - far, send, recv).wait_recv()
 
+    def hand_on(ref, send, recv):
+        to_sibling(ref, (0, pl.ds(0, half - 1)), send, recv.at[0]).wait_recv()
+        to_sibling(ref, far, send, recv.at[1]).start()
+
+    def hand_on_each(ref, send, recv):
+        def step(k):
+            to_sibling(ref, (far, k), send, recv.at[k]).wait_recv()
+            to_sibling(ref, (far, k), send, recv.at[half]).start()
+
+        others(step)
+
     def sent(ref, send, recv):
-        for side, blocks in ((0, half), (1, half - 1)):
-            part_of = ref.at[side, 0:blocks]
+        for kind, blocks in ((0, half), (1, half - 1)):
+            block = ref.at[kind, 0:blocks]
             pltpu.make_async_remote_copy(
-                src_ref=part_of, dst_ref=part_of, send_sem=send.at[side], recv_sem=recv,
+                src_ref=block, dst_ref=block, send_sem=send.at[kind], recv_sem=recv,
                 device_id={"brick": sibling}, device_id_type=MESH,
             ).wait_send()
-
-    def spread_q():
-        repeat(1, lambda j: direct(all_q, j, q_send, q_recv.at[0]).start())
-
-    def hand_on_q():
-        ref = all_q.at[0, 0 : half - 1]
-        pltpu.make_async_remote_copy(
-            src_ref=ref, dst_ref=ref, send_sem=q_send.at[0], recv_sem=q_recv.at[0],
-            device_id={"brick": sibling}, device_id_type=MESH,
-        ).wait_recv()
-        to_sibling(all_q, far, q_send, q_recv.at[1]).start()
-
-    def r_place(j):
-        return far, lax.rem(me // 2 + half - j, half)
-
-    def spread_r():
-        repeat(1, lambda j: direct(all_r, j, r_send, r_recv.at[me // 2]).start())
-        to_sibling(all_r, mine_at, r_send, r_recv.at[half]).start()
-
-    def hand_on_r():
-        def step(j):
-            place = r_place(j)
-            to_sibling(all_r, place, r_send, r_recv.at[place[1]]).wait_recv()
-            to_sibling(all_r, place, r_send, r_recv.at[half]).start()
-
-        repeat(1, step)
 
     def sweep_two(c):
         rows, at = rows_at(c), rows_in(c)
@@ -391,7 +379,7 @@
 
         @pl.when(c == CHUNKS - 1)
         def _():
-            spread_q()
+            spread(all_q, q_send, q_recv.at[0])
 
         @pl.when(c > 0)
         def _():
@@ -438,53 +426,31 @@
 
     lax.fori_loop(0, CHUNKS + 1, second_stage, 0)
 
-    def partial(side):
-        return pltpu.make_async_remote_copy(
-            src_ref=part.at[side],
-            dst_ref=part.at[3 - side],
-            send_sem=part_send.at[side],
-            recv_sem=part_recv.at[1 - side],
-            device_id={"brick": neighbour(side)},
-            device_id_type=MESH,
-        )
-
-    def partial_in(side):
-        return pltpu.make_async_remote_copy(
-            src_ref=part.at[2 + side],
-            dst_ref=part.at[2 + side],
-            send_sem=part_send.at[side],
-            recv_sem=part_recv.at[side],
-            device_id={"brick": neighbour(side)},
-            device_id_type=MESH,
-        )
-
-    for side in range(2):
-        part[side] = to_coarse(ymat[1], zmat[2:4], X[2 * side])
-
-    for side in range(2):
-
-        @pl.when(has[side])
-        def _():
-            partial(side).start()
-
-        @pl.when(jnp.logical_not(has[side]))
-        def _():
-            part[2 + side] = jnp.zeros(part.shape[1:], F32)
-
-    mine = to_coarse(ymat[1], zmat[2:4], X[1])
-    hand_on_q()
-    for side in range(2):
-
-        @pl.when(has[side])
-        def _():
-            partial_in(side).wait_recv()
-
-    all_r[mine_at] = (mine + (part[2] + part[3])) * (1.0 / 64.0)
-    spread_r()
+    restrict = lambda k: to_coarse(ymat[1], zmat[2:4], X[k])
+    all_p[mine_at] = restrict(2 * far)
+    spread(all_p, p_send, p_recv.at[0])
+
+    part[0] = restrict(2 * near_side)
+    swap = pltpu.make_async_remote_copy(
+        src_ref=part.at[0],
+        dst_ref=part.at[1],
+        send_sem=part_sem.at[0],
+        recv_sem=part_sem.at[1],
+        device_id={"brick": sibling},
+        device_id_type=MESH,
+    )
+    swap.start()
+    mine = restrict(1)
+    hand_on(all_q, q_send, q_recv)
+    swap.wait_recv()
+    all_r[mine_at] = mine + part[1]
+    spread(all_r, r_send, r_recv.at[me // 2])
+    to_sibling(all_r, mine_at, r_send, r_recv.at[half]).start()
 
     from_sibling(all_q, q_send, q_recv.at[1])
     coarse_coefficients(n, min(8, n), all_q, q_pad, coef, scaled)
-    hand_on_r()
+    hand_on(all_p, p_send, p_recv)
+    hand_on_each(all_r, r_send, r_recv)
 
     rows, lanes = all_r.shape[2:]
     shifts, _ = coarse_shifts((group, rows, lanes))
@@ -492,9 +458,13 @@
     for slot in range(2):
         C[slot, 0] = edge
         C[slot, n + 1] = edge
+    from_sibling(all_p, p_send, p_recv.at[1])
     from_sibling(all_r, r_send, r_recv.at[half])
     for b in range(n):
-        scaled_rhs = all_r[b % 2, b // 2] * scaled[b]
+        r = all_r[b % 2, b // 2]
+        if 0 < b < n - 1:
+            r = r + all_p[1 - b % 2, b // 2 - 1 + 2 * (b % 2)]
+        scaled_rhs = r * scaled[b]
         B[b] = scaled_rhs
         C[0, b + 1] = scaled_rhs
 
@@ -518,9 +488,10 @@
         @pl.when(has[side])
         def _():
             halo_sent(side).wait_send()
-            partial(side).wait_send()
-
+
+    swap.wait_send()
     sent(all_q, q_send, q_recv.at[0])
+    sent(all_p, p_send, p_recv.at[0])
     sent(all_r, r_send, r_recv.at[0])
 
 
@@ -567,7 +538,7 @@
         for k, out in enumerate((None, None) + outside):
             f = faces[k] * scale
             coef[k, pl.ds(at, group)] = f if out is None else jnp.where(out, 0.0, f)
-        scaled[pl.ds(at, group)] = 16.0 * scale
+        scaled[pl.ds(at, group)] = (16.0 / 64.0) * scale
         return 0
 
     lax.fori_loop(0, n // group, prepare, 0)
@@ -641,14 +612,14 @@
             pltpu.SMEM((n,), jnp.int32),
             whole(6, n, *dense), whole(n, *dense),
             pltpu.VMEM(ymat.shape, BF16), pltpu.VMEM(zmat.shape, BF16),
-            whole(2, n // 2, *dense), whole(n + 2, *dense), whole(2, n // 2, *dense), whole(n, *dense),
+            whole(2, n // 2, *dense), whole(n + 2, *dense), whole(2, n // 2, *dense), whole(2, n // 2, *dense), whole(n, *dense),
             whole(4, ny, nz), whole(4, ny, nz),
             whole(*padded), whole(*padded), whole(*padded),
             whole(4, ny, nz), whole(4, ny, nz), whole(4, ny, nz),
             whole(2, ny, nz), whole(3, ny, nz), whole(3, 2, ny, nz),
-            whole(4, *dense),
-            dma(8), dma(2), dma(2, FIRST), dma(2, CHUNKS), dma(2), dma(2),
-            dma(2), dma(2), dma(2), dma(n // 2 + 1),
+            whole(2, *dense),
+            dma(8), dma(2), dma(2, FIRST), dma(2, CHUNKS), dma(2),
+            dma(2), dma(2), dma(2), dma(2), dma(2), dma(n // 2 + 1),
             pltpu.SemaphoreType.REGULAR(((n - 1).bit_length(),)),
         ],
         compiler_params=pltpu.CompilerParams(

time: 27.2 us -> 25.8 us (0.949)
  Pallas kernels: 26.4 us -> 25 us
    pallas_call x1, Pallas kernels: 25.2 us -> 23.8 us  [local(): pl.pallas_call(functools.partial(smooth_kernel, n, ny, nz, min(16, n)), o...]
where the time goes in v3:
time: 25.8 us; the launch traced here: 25.6 us
  Pallas kernels  25 us (97%)
  between operations  0.64 us (2%)
    pallas_call x1, Pallas kernels, local(): pl.pallas_call(functools.partial(smooth_kernel, n, ny, nz, min(16, n)), o...  23.8 us
    pallas_call x1, Pallas kernels, local(): pl.pallas_call(functools.partial(prolong_kernel, n), out_shape=(jax.Shape...  1.19 us

profile of v3, /device:TPU:1, one launch (start us, length us, event | category | flops | bytes accessed | tf_op | source)
XLA Modules:
  0.0 25.6 jit_solution(6387249242010732510)
XLA Ops:
  0.6 23.8 %smooth.1 = (f32[4,144,256]{2,1,0:T(8,128)S(1)}, f32[2,18,16,128]{3,2,1,0:T(8,128)S(1)}, bf16[2,128,256]{2,1,0:T(8,128)(2,1)S(1)}, bf16[128,32]{1,0:T(8,128)(2,1)S(1)}, s32[16,128]{1,0:T(8,128)S(1)}) custom-call(f32[4,128,256]{2,1,0:T(8,128)} %source_hbm.1, f32[4,128,256]{2,1,0:T(8,128)} %guess_hbm.1, f32[4,128,256]{2,1,0:T(8,128)} %logq_hbm.1, ...), custom_call_target="tpu_custom_call" | custom-call | tf_op jit(solution)/shard_map/smooth/pallas_call | solution.py:603
  24.5 1.2 %prolong.1 = (f32[4,128,256]{2,1,0:T(8,128)}, f32[1,2048]{1,0:T(1,128)}) custom-call(f32[2,18,16,128]{3,2,1,0:T(8,128)S(1)} %get-tuple-element.7.C, f32[4,144,256]{2,1,0:T(8,128)S(1)} %get-tuple-element.8.U2, bf16[2,128,256]{2,1,0:T(8,128)(2,1)S(1)} %get-tuple-element.9.ez, bf16[128,32]{1,0:T(8,128)(2,1)S(1)} %get-tuple-element.10.ey, ...), custom_call_target="tpu_custom_call" | custom-call | tf_op jit(solution)/shard_map/prolong/pallas_call | solution.py:631

commit v4 on v3

--- a/solution.py
+++ b/solution.py
@@ -12,6 +12,7 @@
 SWEEPS = 8
 CHUNKS = 8
 FIRST = 4
+EARLY = 2
 MESH = pl.DeviceIdType.MESH
 F32 = jnp.float32
 BF16 = jnp.bfloat16
@@ -338,20 +339,48 @@
         to_sibling(ref, (0, pl.ds(0, half - 1)), send, recv.at[0]).wait_recv()
         to_sibling(ref, far, send, recv.at[1]).start()
 
+    early = me < EARLY
+
+    def to_early(ref, k, send, recv):
+        return pltpu.make_async_remote_copy(
+            src_ref=ref.at[mine_at],
+            dst_ref=ref.at[mine_at],
+            send_sem=send.at[2],
+            recv_sem=recv,
+            device_id={"brick": 2 * k + 1 - far},
+            device_id_type=MESH,
+        )
+
+    def spread_early(ref, send, recv):
+        for k in range(EARLY // 2):
+
+            @pl.when(me // 2 != k)
+            def _():
+                to_early(ref, k, send, recv.at[half]).start()
+
     def hand_on_each(ref, send, recv):
         def step(k):
             to_sibling(ref, (far, k), send, recv.at[k]).wait_recv()
-            to_sibling(ref, (far, k), send, recv.at[half]).start()
+
+            @pl.when(jnp.logical_not(early))
+            def _():
+                to_sibling(ref, (far, k), send, recv.at[half]).start()
 
         others(step)
 
-    def sent(ref, send, recv):
-        for kind, blocks in ((0, half), (1, half - 1)):
-            block = ref.at[kind, 0:blocks]
-            pltpu.make_async_remote_copy(
-                src_ref=block, dst_ref=block, send_sem=send.at[kind], recv_sem=recv,
-                device_id={"brick": sibling}, device_id_type=MESH,
-            ).wait_send()
+    def sent_early(ref, send, recv):
+        for k in range(EARLY // 2):
+
+            @pl.when(me // 2 != k)
+            def _():
+                to_early(ref, k, send, recv.at[half]).wait_send()
+
+    def sent(ref, kind, blocks, send, recv):
+        block = ref.at[kind, 0:blocks]
+        pltpu.make_async_remote_copy(
+            src_ref=block, dst_ref=block, send_sem=send.at[kind], recv_sem=recv,
+            device_id={"brick": sibling}, device_id_type=MESH,
+        ).wait_send()
 
     def sweep_two(c):
         rows, at = rows_at(c), rows_in(c)
@@ -444,6 +473,7 @@
     hand_on(all_q, q_send, q_recv)
     swap.wait_recv()
     all_r[mine_at] = mine + part[1]
+    spread_early(all_r, r_send, r_recv)
     spread(all_r, r_send, r_recv.at[me // 2])
     to_sibling(all_r, mine_at, r_send, r_recv.at[half]).start()
 
@@ -490,9 +520,20 @@
             halo_sent(side).wait_send()
 
     swap.wait_send()
-    sent(all_q, q_send, q_recv.at[0])
-    sent(all_p, p_send, p_recv.at[0])
-    sent(all_r, r_send, r_recv.at[0])
+    sent(all_q, 0, half, q_send, q_recv.at[0])
+    sent(all_p, 0, half, p_send, p_recv.at[0])
+    for ref, send, recv in ((all_q, q_send, q_recv), (all_p, p_send, p_recv), (all_r, r_send, r_recv)):
+        sent(ref, 1, half - 1, send, recv.at[0])
+
+    @pl.when(early)
+    def _():
+        sent(all_r, 0, 1, r_send, r_recv.at[0])
+
+    @pl.when(jnp.logical_not(early))
+    def _():
+        sent(all_r, 0, half, r_send, r_recv.at[0])
+
+    sent_early(all_r, r_send, r_recv)
 
 
 def coarse_shifts(shape):
@@ -619,7 +660,7 @@
             whole(2, ny, nz), whole(3, ny, nz), whole(3, 2, ny, nz),
             whole(2, *dense),
             dma(8), dma(2), dma(2, FIRST), dma(2, CHUNKS), dma(2),
-            dma(2), dma(2), dma(2), dma(2), dma(2), dma(n // 2 + 1),
+            dma(2), dma(2), dma(2), dma(2), dma(3), dma(n // 2 + 1),
             pltpu.SemaphoreType.REGULAR(((n - 1).bit_length(),)),
         ],
         compiler_params=pltpu.CompilerParams(

time: 25.8 us -> 25.3 us (0.981)
  Pallas kernels: 25 us -> 24.5 us
    pallas_call x1, Pallas kernels: 23.8 us -> 23.3 us  [local(): pl.pallas_call(functools.partial(smooth_kernel, n, ny, nz, min(16, n)), o...]
where the time goes in v4:
time: 25.3 us; the launch traced here: 25.1 us
  Pallas kernels  24.5 us (97%)
  between operations  0.64 us (3%)
    pallas_call x1, Pallas kernels, local(): pl.pallas_call(functools.partial(smooth_kernel, n, ny, nz, min(16, n)), o...  23.3 us
    pallas_call x1, Pallas kernels, local(): pl.pallas_call(functools.partial(prolong_kernel, n), out_shape=(jax.Shape...  1.19 us

profile of v4, /device:TPU:1, one launch (start us, length us, event | category | flops | bytes accessed | tf_op | source)
XLA Modules:
  0.0 25.1 jit_solution(1174508760827721805)
XLA Ops:
  0.6 23.3 %smooth.1 = (f32[4,144,256]{2,1,0:T(8,128)S(1)}, f32[2,18,16,128]{3,2,1,0:T(8,128)S(1)}, bf16[2,128,256]{2,1,0:T(8,128)(2,1)S(1)}, bf16[128,32]{1,0:T(8,128)(2,1)S(1)}, s32[16,128]{1,0:T(8,128)S(1)}) custom-call(f32[4,128,256]{2,1,0:T(8,128)} %source_hbm.1, f32[4,128,256]{2,1,0:T(8,128)} %guess_hbm.1, f32[4,128,256]{2,1,0:T(8,128)} %logq_hbm.1, ...), custom_call_target="tpu_custom_call" | custom-call | tf_op jit(solution)/shard_map/smooth/pallas_call | solution.py:644
  23.9 1.2 %prolong.1 = (f32[4,128,256]{2,1,0:T(8,128)}, f32[1,2048]{1,0:T(1,128)}) custom-call(f32[2,18,16,128]{3,2,1,0:T(8,128)S(1)} %get-tuple-element.7.C, f32[4,144,256]{2,1,0:T(8,128)S(1)} %get-tuple-element.8.U2, bf16[2,128,256]{2,1,0:T(8,128)(2,1)S(1)} %get-tuple-element.9.ez, bf16[128,32]{1,0:T(8,128)(2,1)S(1)} %get-tuple-element.10.ey, ...), custom_call_target="tpu_custom_call" | custom-call | tf_op jit(solution)/shard_map/prolong/pallas_call | solution.py:672

commit v5 on v4

--- a/solution.py
+++ b/solution.py
@@ -13,6 +13,8 @@
 CHUNKS = 8
 FIRST = 4
 EARLY = 2
+HELD = 2
+RELEASE = (4, 7)
 MESH = pl.DeviceIdType.MESH
 F32 = jnp.float32
 BF16 = jnp.bfloat16
@@ -145,8 +147,8 @@
 
     Q = ny // FIRST
 
-    def send_first(side):
-        for c in range(FIRST):
+    def send_first(side, chunks):
+        for c in chunks:
             rows = pl.ds(c * Q, Q)
             for which, ref in enumerate((logq_hbm, guess_hbm)):
                 pltpu.make_async_remote_copy(
@@ -201,11 +203,17 @@
             device_id_type=MESH,
         )
 
-    for side in (far, near_side):
-
-        @pl.when(exists(side))
-        def _():
-            send_first(side)
+    holds = jnp.logical_and(lax.rem(me + 1, 4) < 2, exists(far)) if n == 16 else False
+
+    @pl.when(exists(far))
+    def _():
+        send_first(far, range(HELD))
+
+    @pl.when(jnp.logical_and(exists(far), jnp.logical_not(holds)))
+    def _():
+        send_first(far, range(HELD, FIRST))
+
+    send_first(near_side, range(FIRST))
 
     relay(0)
 
@@ -250,6 +258,12 @@
         return [0.5 * (middle(k[p]) * across(u, p) + across(uk, p)) for p in range(4)]
 
     def sweep_one(c, _):
+        for k, at_step in enumerate(RELEASE):
+
+            @pl.when(jnp.logical_and(holds, c == at_step))
+            def _():
+                send_first(far, [HELD + k])
+
         rows, at = rows_at(c), rows_in(c)
         u, k = windows(U0, c), windows(K, c)
         near = nearby(u, k)

time: 25.3 us -> 24.6 us (0.972)
  Pallas kernels: 24.5 us -> 23.6 us
    pallas_call x1, Pallas kernels: 23.3 us -> 22.5 us  [local(): pl.pallas_call(functools.partial(smooth_kernel, n, ny, nz, min(16, n)), o...]
where the time goes in v5:
time: 24.6 us; the launch traced here: 24.3 us
  Pallas kernels  23.6 us (96%)
  between operations  0.64 us (3%)
    pallas_call x1, Pallas kernels, local(): pl.pallas_call(functools.partial(smooth_kernel, n, ny, nz, min(16, n)), o...  22.5 us
    pallas_call x1, Pallas kernels, local(): pl.pallas_call(functools.partial(prolong_kernel, n), out_shape=(jax.Shape...  1.19 us

profile of v5, /device:TPU:1, one launch (start us, length us, event | category | flops | bytes accessed | tf_op | source)
XLA Modules:
  0.0 24.3 jit_solution(13722936035467947138)
XLA Ops:
  0.6 22.5 %smooth.1 = (f32[4,144,256]{2,1,0:T(8,128)S(1)}, f32[2,18,16,128]{3,2,1,0:T(8,128)S(1)}, bf16[2,128,256]{2,1,0:T(8,128)(2,1)S(1)}, bf16[128,32]{1,0:T(8,128)(2,1)S(1)}, s32[16,128]{1,0:T(8,128)S(1)}) custom-call(f32[4,128,256]{2,1,0:T(8,128)} %source_hbm.1, f32[4,128,256]{2,1,0:T(8,128)} %guess_hbm.1, f32[4,128,256]{2,1,0:T(8,128)} %logq_hbm.1, ...), custom_call_target="tpu_custom_call" | custom-call | tf_op jit(solution)/shard_map/smooth/pallas_call | solution.py:658
  23.1 1.2 %prolong.1 = (f32[4,128,256]{2,1,0:T(8,128)}, f32[1,2048]{1,0:T(1,128)}) custom-call(f32[2,18,16,128]{3,2,1,0:T(8,128)S(1)} %get-tuple-element.7.C, f32[4,144,256]{2,1,0:T(8,128)S(1)} %get-tuple-element.8.U2, bf16[2,128,256]{2,1,0:T(8,128)(2,1)S(1)} %get-tuple-element.9.ez, bf16[128,32]{1,0:T(8,128)(2,1)S(1)} %get-tuple-element.10.ey, ...), custom_call_target="tpu_custom_call" | custom-call | tf_op jit(solution)/shard_map/prolong/pallas_call | solution.py:686

commit v6 on v5

--- a/solution.py
+++ b/solution.py
@@ -420,10 +420,6 @@
             def _():
                 relay(k)
 
-        @pl.when(c == CHUNKS - 1)
-        def _():
-            spread(all_q, q_send, q_recv.at[0])
-
         @pl.when(c > 0)
         def _():
             sweep_two(c - 1)
@@ -457,6 +453,10 @@
         X[2, rows] = 0.625 * fhi + 0.375 * r[3] + 0.125 * r[2]
 
     def second_stage(c, _):
+        @pl.when(c == 3)
+        def _():
+            spread(all_q, q_send, q_recv.at[0])
+
         @pl.when(c < CHUNKS)
         def _():
             finish_two(c)

time: 24.6 us -> 24.5 us (level)
  no operation moved by 1% of the time
where the time goes in v6:
time: 24.5 us; the launch traced here: 24.1 us
  Pallas kernels  23.5 us (96%)
  between operations  0.64 us (3%)
    pallas_call x1, Pallas kernels, local(): pl.pallas_call(functools.partial(smooth_kernel, n, ny, nz, min(16, n)), o...  22.3 us
    pallas_call x1, Pallas kernels, local(): pl.pallas_call(functools.partial(prolong_kernel, n), out_shape=(jax.Shape...  1.19 us

profile of v6, /device:TPU:1, one launch (start us, length us, event | category | flops | bytes accessed | tf_op | source)
XLA Modules:
  0.0 24.1 jit_solution(1610189263084044164)
XLA Ops:
  0.6 22.3 %smooth.1 = (f32[4,144,256]{2,1,0:T(8,128)S(1)}, f32[2,18,16,128]{3,2,1,0:T(8,128)S(1)}, bf16[2,128,256]{2,1,0:T(8,128)(2,1)S(1)}, bf16[128,32]{1,0:T(8,128)(2,1)S(1)}, s32[16,128]{1,0:T(8,128)S(1)}) custom-call(f32[4,128,256]{2,1,0:T(8,128)} %source_hbm.1, f32[4,128,256]{2,1,0:T(8,128)} %guess_hbm.1, f32[4,128,256]{2,1,0:T(8,128)} %logq_hbm.1, ...), custom_call_target="tpu_custom_call" | custom-call | tf_op jit(solution)/shard_map/smooth/pallas_call | solution.py:658
  23.0 1.2 %prolong.1 = (f32[4,128,256]{2,1,0:T(8,128)}, f32[1,2048]{1,0:T(1,128)}) custom-call(f32[2,18,16,128]{3,2,1,0:T(8,128)S(1)} %get-tuple-element.7.C, f32[4,144,256]{2,1,0:T(8,128)S(1)} %get-tuple-element.8.U2, bf16[2,128,256]{2,1,0:T(8,128)(2,1)S(1)} %get-tuple-element.9.ez, bf16[128,32]{1,0:T(8,128)(2,1)S(1)} %get-tuple-element.10.ey, ...), custom_call_target="tpu_custom_call" | custom-call | tf_op jit(solution)/shard_map/prolong/pallas_call | solution.py:686

commit v7 on v6

--- a/solution.py
+++ b/solution.py
@@ -487,9 +487,9 @@
     hand_on(all_q, q_send, q_recv)
     swap.wait_recv()
     all_r[mine_at] = mine + part[1]
+    to_sibling(all_r, mine_at, r_send, r_recv.at[half]).start()
     spread_early(all_r, r_send, r_recv)
     spread(all_r, r_send, r_recv.at[me // 2])
-    to_sibling(all_r, mine_at, r_send, r_recv.at[half]).start()
 
     from_sibling(all_q, q_send, q_recv.at[1])
     coarse_coefficients(n, min(8, n), all_q, q_pad, coef, scaled)
@@ -614,16 +614,14 @@
         ],
         axis=0,
     )
-    hi, lo = split(planes)
-    even = dot(hi, ez[0]) + dot(lo, ez[0])
-    odd = dot(hi, ez[1]) + dot(lo, ez[1])
+    pair = jnp.concatenate(split(planes), axis=1)
+    even, odd = dot(pair, ez[0]), dot(pair, ez[1])
     copies = []
     for p in range(4):
         both = jnp.concatenate(
             [even[p * rows : (p + 1) * rows], odd[p * rows : (p + 1) * rows]], axis=0
         )
-        hi, lo = split(both)
-        corrected[p] = U2[p, 8 : ny + 8] + (dot(ey[...], hi) + dot(ey[...], lo))
+        corrected[p] = U2[p, 8 : ny + 8] + dot(ey[...], jnp.concatenate(split(both), axis=0))
         copies.append(pltpu.make_async_copy(corrected.at[p], corrected_hbm.at[p], sem.at[p]))
         copies[p].start()
 
@@ -649,7 +647,8 @@
     py, pz = even_odd(prolong_matrix(ny)), prolong_matrix(nz)
     ymat = as_bf16(np.stack([even_odd(mean_matrix(ny)).T, py.T]))
     zmat = as_bf16(np.concatenate([halves(mean_matrix(nz)), halves(pz)]))
-    ey, ez = as_bf16(py), as_bf16(halves(pz).transpose(0, 2, 1))
+    ey = as_bf16(np.concatenate([py, py], 1))
+    ez = as_bf16(np.concatenate([halves(pz).transpose(0, 2, 1)] * 2, 1))
     vmem = pl.BlockSpec(memory_space=pltpu.VMEM)
     hbm = pl.BlockSpec(memory_space=pl.ANY)
     whole = lambda *s: pltpu.VMEM(s, F32)

time: 24.5 us -> 24.4 us (level)
  no operation moved by 1% of the time
where the time goes in v7:
time: 24.4 us; the launch traced here: 24.1 us
  Pallas kernels  23.5 us (96%)
  between operations  0.64 us (3%)
    pallas_call x1, Pallas kernels, local(): pl.pallas_call(functools.partial(smooth_kernel, n, ny, nz, min(16, n)), o...  22.3 us
    pallas_call x1, Pallas kernels, local(): pl.pallas_call(functools.partial(prolong_kernel, n), out_shape=(jax.Shape...  1.16 us

profile of v7, /device:TPU:1, one launch (start us, length us, event | category | flops | bytes accessed | tf_op | source)
XLA Modules:
  0.0 24.1 jit_solution(16029858227718845870)
XLA Ops:
  0.6 22.3 %smooth.1 = (f32[4,144,256]{2,1,0:T(8,128)S(1)}, f32[2,18,16,128]{3,2,1,0:T(8,128)S(1)}, bf16[2,256,256]{2,1,0:T(8,128)(2,1)S(1)}, bf16[128,64]{1,0:T(8,128)(2,1)S(1)}, s32[16,128]{1,0:T(8,128)S(1)}) custom-call(f32[4,128,256]{2,1,0:T(8,128)} %source_hbm.1, f32[4,128,256]{2,1,0:T(8,128)} %guess_hbm.1, f32[4,128,256]{2,1,0:T(8,128)} %logq_hbm.1, ...), custom_call_target="tpu_custom_call" | custom-call | tf_op jit(solution)/shard_map/smooth/pallas_call | solution.py:657
  23.0 1.2 %prolong.1 = (f32[4,128,256]{2,1,0:T(8,128)}, f32[1,2048]{1,0:T(1,128)}) custom-call(f32[2,18,16,128]{3,2,1,0:T(8,128)S(1)} %get-tuple-element.7.C, f32[4,144,256]{2,1,0:T(8,128)S(1)} %get-tuple-element.8.U2, bf16[2,256,256]{2,1,0:T(8,128)(2,1)S(1)} %get-tuple-element.9.ez, bf16[128,64]{1,0:T(8,128)(2,1)S(1)} %get-tuple-element.10.ey, ...), custom_call_target="tpu_custom_call" | custom-call | tf_op jit(solution)/shard_map/prolong/pallas_call | solution.py:685

commit v8 on v7

--- a/solution.py
+++ b/solution.py
@@ -79,6 +79,7 @@
     near_side = 1 - far
     sibling = me + 1 - 2 * far
     mine_at = (far, me // 2)
+    at_end = jnp.logical_or(me == 0, me == n - 1)
     neighbour = lambda side: me - 1 + 2 * side
     exists = lambda side: jnp.logical_and(neighbour(side) >= 0, neighbour(side) < n)
 
@@ -119,6 +120,9 @@
             greeted(token_sem.at[k], distances[k])
         if k + 1 < len(distances):
             greet(token_sem.at[k + 1], distances[k + 1])
+
+    for place in ((0, 0), (1, half - 1)):
+        all_p[place] = jnp.zeros(all_p.shape[2:], F32)
 
     greet(barrier, 1)
     for copy in loads:
@@ -453,7 +457,7 @@
         X[2, rows] = 0.625 * fhi + 0.375 * r[3] + 0.125 * r[2]
 
     def second_stage(c, _):
-        @pl.when(c == 3)
+        @pl.when(c == jnp.where(me < n // 2, 3, 2))
         def _():
             spread(all_q, q_send, q_recv.at[0])
 
@@ -471,7 +475,7 @@
 
     restrict = lambda k: to_coarse(ymat[1], zmat[2:4], X[k])
     all_p[mine_at] = restrict(2 * far)
-    spread(all_p, p_send, p_recv.at[0])
+    pl.when(jnp.logical_not(at_end))(lambda: spread(all_p, p_send, p_recv.at[0]))
 
     part[0] = restrict(2 * near_side)
     swap = pltpu.make_async_remote_copy(
@@ -493,7 +497,13 @@
 
     from_sibling(all_q, q_send, q_recv.at[1])
     coarse_coefficients(n, min(8, n), all_q, q_pad, coef, scaled)
-    hand_on(all_p, p_send, p_recv)
+    for ended, blocks in ((at_end, half - 1), (jnp.logical_not(at_end), half - 2)):
+
+        @pl.when(ended)
+        def _():
+            to_sibling(all_p, (0, pl.ds(0, blocks)), p_send, p_recv.at[0]).wait_recv()
+
+    to_sibling(all_p, far, p_send, p_recv.at[1]).start()
     hand_on_each(all_r, r_send, r_recv)
 
     rows, lanes = all_r.shape[2:]
@@ -536,8 +546,9 @@
     swap.wait_send()
     sent(all_q, 0, half, q_send, q_recv.at[0])
     sent(all_p, 0, half, p_send, p_recv.at[0])
-    for ref, send, recv in ((all_q, q_send, q_recv), (all_p, p_send, p_recv), (all_r, r_send, r_recv)):
+    for ref, send, recv in ((all_q, q_send, q_recv), (all_r, r_send, r_recv)):
         sent(ref, 1, half - 1, send, recv.at[0])
+    pl.when(jnp.logical_not(at_end))(lambda: sent(all_p, 1, half - 1, p_send, p_recv.at[0]))
 
     @pl.when(early)
     def _():

time: 24.4 us -> 24.3 us (level)
  no operation moved by 1% of the time
where the time goes in v8:
time: 24.3 us; the launch traced here: 24 us
  Pallas kernels  23.4 us (96%)
  between operations  0.64 us (3%)
    pallas_call x1, Pallas kernels, local(): pl.pallas_call(functools.partial(smooth_kernel, n, ny, nz, min(16, n)), o...  22.2 us
    pallas_call x1, Pallas kernels, local(): pl.pallas_call(functools.partial(prolong_kernel, n), out_shape=(jax.Shape...  1.16 us

profile of v8, /device:TPU:1, one launch (start us, length us, event | category | flops | bytes accessed | tf_op | source)
XLA Modules:
  0.0 24.0 jit_solution(2316218364460090143)
XLA Ops:
  0.6 22.2 %smooth.1 = (f32[4,144,256]{2,1,0:T(8,128)S(1)}, f32[2,18,16,128]{3,2,1,0:T(8,128)S(1)}, bf16[2,256,256]{2,1,0:T(8,128)(2,1)S(1)}, bf16[128,64]{1,0:T(8,128)(2,1)S(1)}, s32[16,128]{1,0:T(8,128)S(1)}) custom-call(f32[4,128,256]{2,1,0:T(8,128)} %source_hbm.1, f32[4,128,256]{2,1,0:T(8,128)} %guess_hbm.1, f32[4,128,256]{2,1,0:T(8,128)} %logq_hbm.1, ...), custom_call_target="tpu_custom_call" | custom-call | tf_op jit(solution)/shard_map/smooth/pallas_call | solution.py:668
  22.9 1.2 %prolong.1 = (f32[4,128,256]{2,1,0:T(8,128)}, f32[1,2048]{1,0:T(1,128)}) custom-call(f32[2,18,16,128]{3,2,1,0:T(8,128)S(1)} %get-tuple-element.7.C, f32[4,144,256]{2,1,0:T(8,128)S(1)} %get-tuple-element.8.U2, bf16[2,256,256]{2,1,0:T(8,128)(2,1)S(1)} %get-tuple-element.9.ez, bf16[128,64]{1,0:T(8,128)(2,1)S(1)} %get-tuple-element.10.ey, ...), custom_call_target="tpu_custom_call" | custom-call | tf_op jit(solution)/shard_map/prolong/pallas_call | solution.py:696
